TPU v7x, 256 devices: a whole 4x4x8 slice. The times are simulated.
256 devices in a mesh: seq: 64 (over z, x, core), mlp: 4 (over y).
Axes of the slice: x: 4, y: 4, z: 8, core: 2. Of those that a mesh axis runs over, the one named last changes fastest.
Arguments:
- tokens: bfloat16 [32768, 1024], P('seq'), may hold values from -6 to 6
- positions: int32 [4096], replicated, may hold values from 0 to 32767, as said below
- value_proj: bfloat16 [1024, 1024], replicated, may hold values from -0.1875 to 0.1875
- write_proj: bfloat16 [1024, 128], replicated, may hold values from -0.1875 to 0.1875
- read_proj: bfloat16 [1024, 128], replicated, may hold values from -0.1875 to 0.1875
- step_proj: bfloat16 [1024, 16], replicated, may hold values from -0.1875 to 0.1875
- step_bias: float32 [16], replicated, may hold values from -1 to 1
- decay_rate: float32 [16], replicated, may hold values from 6.1035156e-06 to 0.035, as said below
- reset_depth: float32 [32768], P('seq'), may hold values from 0 to 0.7, as said below
- out_proj: bfloat16 [1024, 1024], replicated, may hold values from -0.1875 to 0.1875
- router: float32 [1024], replicated, may hold values from -0.1875 to 0.1875
- pad_vector: bfloat16 [1024], replicated, may hold values from -6 to 6
- up_weight: bfloat16 [2048, 4096], P(None, 'mlp'), may hold values from -0.125 to 0.125
- down_weight: bfloat16 [1024, 4096], P(None, 'mlp'), may hold values from -0.09375 to 0.09375
- cotangent: bfloat16 [32768, 1024], P('seq'), may hold values from -16 to 16
Outputs:
- mixed: bfloat16 [32768, 1024], P('seq')
- up_grad: float32 [2048, 4096], P('seq', 'mlp')
- down_grad: float32 [1024, 4096], P('seq', 'mlp')
Inputs may be any that keep to these rules, and one draw needn't show every extreme that they name: `positions`: strictly increasing; every multiple of 512 is among them; each aligned block of 512 bytes holds between 1 and 127 of them, and both counts are reached. `decay_rate`: positive rates. `reset_depth`: Nonnegative.
All inputs are finite; a program needn't handle non-finite values.
Results may differ from a plain program's by a relative error of at most 0.017.
Values may be sent and summed in bfloat16 or wider, within the bound.
A program may use at most 128 MiB of HBM per device.

v0:
```python
import jax
import jax.numpy as jnp
from jax import lax
from jax.sharding import PartitionSpec as P

HIGHEST = lax.Precision.HIGHEST


def carried_in(x, axis, combine, identity):
    peers, here = (lax.axis_size(axis), lax.axis_index(axis))
    everything = jax.tree.map(lambda part: lax.all_gather(part, axis), x)
    start = jax.tree.map(
        lambda part, zero: jnp.broadcast_to(jnp.asarray(zero, part.dtype), part.shape), x, identity
    )

    def step(k, before):
        reached = k < here
        new = combine(before, jax.tree.map(lambda part: part[k], everything))
        return jax.tree.map(lambda a, b: jnp.where(reached, a, b), new, before)

    return lax.fori_loop(0, peers, step, start)


def norm_rows(field):
    return field * lax.rsqrt(jnp.mean(field * field, axis=-1, keepdims=True) + 1e-05)


def smooth_gate(field):
    return jax.nn.gelu(field, approximate=True)


def block_terms(values, write_keys, read_keys, step_size, log_decay):
    cum_decay = jnp.cumsum(log_decay, axis=0)
    scores = lax.dot_general(
        read_keys, write_keys, (((1,), (1,)), ((), ())), preferred_element_type=jnp.float32
    )
    step_ids = jnp.arange(log_decay.shape[0])
    causal = step_ids[:, None] >= step_ids[None, :]
    log_gap = cum_decay[:, None, :] - cum_decay[None, :, :]
    decays = jnp.exp(jnp.where(causal[:, :, None], log_gap, -jnp.inf))
    mixing = scores[:, :, None] * decays
    weighted = step_size[:, :, None] * values.astype(jnp.float32)
    within = jnp.einsum("tsh,shp->thp", mixing, weighted, precision=HIGHEST)
    tail_weight = jnp.exp(cum_decay[-1][None, :] - cum_decay) * step_size
    fresh_state = jnp.einsum(
        "shp,sn->hpn",
        tail_weight[:, :, None] * values.astype(jnp.float32),
        write_keys.astype(jnp.float32),
        precision=HIGHEST,
    )
    return (within, cum_decay, jnp.exp(cum_decay[-1]), fresh_state)


def carried_terms(ssd_state, read_keys, cum_decay):
    return jnp.exp(cum_decay)[:, :, None] * jnp.einsum(
        "hpn,tn->thp", ssd_state, read_keys.astype(jnp.float32), precision=HIGHEST
    )


def combine(before, behind):
    return (before[0] * behind[0], behind[0][:, None, None] * before[1] + behind[1])


def inner_layer(group_rows, group_grad, pad_vector, up_weight, down_weight):
    row_count = group_rows.shape[0]
    widened = jnp.concatenate(
        [group_rows, jnp.broadcast_to(pad_vector, (row_count, pad_vector.shape[0]))], axis=1
    )
    inner_normed = norm_rows(widened.astype(jnp.float32)).astype(jnp.bfloat16)
    hidden_pre = jnp.dot(inner_normed, up_weight, preferred_element_type=jnp.float32)
    hidden = smooth_gate(hidden_pre).astype(jnp.bfloat16)
    partial_value = lax.dot_general(
        hidden, down_weight, (((1,), (1,)), ((), ())), preferred_element_type=jnp.float32
    )
    summed = lax.psum(partial_value, "mlp")
    inner_out = (group_rows.astype(jnp.float32) + summed).astype(jnp.bfloat16)
    hidden_grad = jnp.dot(group_grad, down_weight, preferred_element_type=jnp.float32)
    unused, pull_back = jax.vjp(smooth_gate, hidden_pre)
    pre_grad = pull_back(hidden_grad)[0].astype(jnp.bfloat16)
    return (inner_out, inner_normed, hidden, pre_grad)


def weight_grads(inner_normed, group_grad, hidden, pre_grad):
    up_term = lax.dot_general(
        inner_normed, pre_grad, (((0,), (0,)), ((), ())), preferred_element_type=jnp.float32
    )
    down_term = lax.dot_general(
        group_grad, hidden, (((0,), (0,)), ((), ())), preferred_element_type=jnp.float32
    )
    up_grad, down_grad = (
        lax.psum_scatter(up_term, "seq", scatter_dimension=0, tiled=True),
        lax.psum_scatter(down_term, "seq", scatter_dimension=0, tiled=True),
    )
    return (up_grad, down_grad)


def on_device(
    tokens,
    positions,
    value_proj,
    write_proj,
    read_proj,
    step_proj,
    step_bias,
    decay_rate,
    reset_depth,
    out_proj,
    router,
    pad_vector,
    up_weight,
    down_weight,
    cotangent,
):
    row_count = tokens.shape[0]
    head_count = decay_rate.shape[0]
    head_size = value_proj.shape[1] // head_count
    seq_count = lax.axis_size("seq")
    my_index = lax.axis_index("seq")
    wide_tokens = tokens.astype(jnp.float32)
    normed = norm_rows(wide_tokens).astype(jnp.bfloat16)
    values = jnp.dot(normed, value_proj, preferred_element_type=jnp.float32).astype(jnp.bfloat16)
    values = values.reshape(row_count, head_count, head_size)
    write_keys = jnp.dot(normed, write_proj, preferred_element_type=jnp.float32).astype(
        jnp.bfloat16
    )
    read_keys = jnp.dot(normed, read_proj, preferred_element_type=jnp.float32).astype(jnp.bfloat16)
    step_size = jax.nn.softplus(
        jnp.dot(normed, step_proj, preferred_element_type=jnp.float32) + step_bias
    )
    log_decay = -step_size * decay_rate - reset_depth[:, None]
    within, cum_decay, block_decay, fresh_state = block_terms(
        values, write_keys, read_keys, step_size, log_decay
    )
    identity = (jnp.ones((head_count,), jnp.float32), jnp.zeros_like(fresh_state))
    incoming = carried_in((block_decay, fresh_state), "seq", combine, identity)
    scanned = within + carried_terms(incoming[1], read_keys, cum_decay)
    scan_normed = norm_rows(scanned.reshape(row_count, head_count * head_size)).astype(jnp.bfloat16)
    encoded = (
        wide_tokens + jnp.dot(scan_normed, out_proj, preferred_element_type=jnp.float32)
    ).astype(jnp.bfloat16)
    encoded_f32 = encoded.astype(jnp.float32)
    confidence = jax.nn.sigmoid(jnp.dot(encoded_f32, router, precision=HIGHEST))
    per_device = positions.shape[0] // seq_count
    slot_count = -(-2 * per_device // seq_count)
    capacity = seq_count * slot_count
    bounds = jnp.arange(seq_count + 1, dtype=jnp.int32) * row_count
    starts = jnp.sum((positions[None, :] < bounds[:, None]).astype(jnp.int32), axis=1)
    first = starts[my_index]
    group_count = starts[my_index + 1] - first
    padded = jnp.concatenate([positions, jnp.full((capacity,), row_count * seq_count, jnp.int32)])
    local_starts = lax.dynamic_slice_in_dim(padded, first, capacity)
    slot_ids = jnp.arange(capacity, dtype=jnp.int32)
    is_valid = slot_ids < group_count
    offsets = jnp.where(is_valid, local_starts - my_index * row_count, 0)
    group_rows = jnp.where(is_valid[:, None], encoded[offsets], jnp.zeros((), jnp.bfloat16))
    byte_pos = jnp.arange(row_count, dtype=jnp.int32) + my_index * row_count
    group_of = (
        jnp.sum(
            (is_valid[None, :] & (local_starts[None, :] <= byte_pos[:, None])).astype(jnp.int32),
            axis=1,
        )
        - 1
    )
    member = (group_of[None, :] == slot_ids[:, None]).astype(jnp.float32)
    group_grad = jnp.dot(
        member, confidence[:, None] * cotangent.astype(jnp.float32), precision=HIGHEST
    ).astype(jnp.bfloat16)
    inner_out, inner_normed, hidden, pre_grad = inner_layer(
        group_rows, group_grad, pad_vector, up_weight, down_weight
    )
    mixed = (encoded_f32 + confidence[:, None] * inner_out[group_of].astype(jnp.float32)).astype(
        jnp.bfloat16
    )
    up_grad, down_grad = weight_grads(inner_normed, group_grad, hidden, pre_grad)
    return (mixed, up_grad, down_grad)


def solution(mesh):
    placed = (
        P("seq", None),
        P(),
        P(),
        P(),
        P(),
        P(),
        P(),
        P(),
        P("seq"),
        P(),
        P(),
        P(),
        P(None, "mlp"),
        P(None, "mlp"),
        P("seq", None),
    )
    return jax.shard_map(
        on_device,
        mesh=mesh,
        in_specs=placed,
        out_specs=(P("seq", None), P("seq", "mlp"), P("seq", "mlp")),
        check_vma=False,
    )
```

profile of v0, /device:TPU:32, one launch (start us, length us, event | category | flops | bytes accessed | tf_op | source)
XLA Modules:
  0.0 618.1 jit_solution(14071337181668428780)
XLA Ops:
  7.3 1.7 fusion.11
  8.9 1.7 convolution_add_fusion
  12.4 1.4 convolution_convert_fusion.1
  13.9 4.2 fusion.21
  18.1 2.9 copy.28
  21.0 3.5 fusion.18
  28.7 41.2 %all-gather.1 = f32[64,1,16]{2,1,0:T(1,128)S(1)} all-gather(f32[1,1,16]{2,1,0:T(1,128)S(1)} %bitcast.98), channel_id=1, replica_groups=mesh['seq'=64,'mlp'=4] {'seq'}, dimensions={0}, use_global_device_ids=true | all-gather | bytes 4160 | tf_op jit(solution)/shard_map/all_gather | solution.py:11
  70.3 1.8 convolution_convert_fusion.2
  72.4 19.6 %fusion.1 = f32[16,64,512]{2,1,0:T(8,128)} fusion(f32[512,16]{0,1:T(8,128)S(1)} %bitcast_bitcast_fusion, f32[512,512]{1,0:T(8,128)S(1)} %fusion.78, pred[512,512]{1,0:T(8,128)(4,1)S(1)} %iota_compare_fusion, f32[512,16,64]{0,2,1:T(8,128)S(1)} %bitcast.90, f32[512,16]{0,1:T(8,128)S(1)} %get-tuple-element.132), kind=kOutput, calls=%fused_computation.5 | convolution fusion | flops 3234332672 | bytes 5570560 | tf_op jit(solution)/shard_map/tsh,shp->thp/dot_general | solution.py:43
  92.0 75.5 %all-gather.4.cloned.1.call-done = f32[1024,64,128]{2,1,0:T(8,128)} async-done(((f32[16,64,128]{2,1,0:T(8,128)}), f32[1024,64,128]{2,1,0:T(8,128)}) %all-gather.4.cloned.1.call-update) | async-done | bytes 33554448 | tf_op jit(solution)/shard_map/all_gather | solution.py:11
  167.6 78.1 %while.14 = (s32[]{:T(128)}, f32[16,64,128]{2,1,0:T(8,128)S(1)}, s32[]{:T(128)}, f32[64,16]{1,0:T(8,128)S(1)}, f32[64,16,64,128]{3,2,1,0:T(8,128)}, /*index=5*/s32[]{:T(128)}, s32[]{:T(128)}) while((s32[]{:T(128)}, f32[16,64,128]{2,1,0:T(8,128)S(1)}, s32[]{:T(128)}, f32[64,16]{1,0:T(8,128)S(1)}, f32[64,16,64,128]{3,2,1,0:T(8,128)}, ...), condition=%wide.region_4.5_spmd.clone, body=%wide.region_3.4_spmd.clone.sunk | while | flops 524292 | bytes 1573169 | solution.py:21
  168.8 1.2 fusion.98
  170.0 1.2 fusion.98
  171.2 1.2 fusion.98
  172.4 1.2 fusion.98
  173.6 1.2 fusion.98
  174.9 1.2 fusion.98
  176.1 1.2 fusion.98
  177.3 1.2 fusion.98
  178.5 1.2 fusion.98
  179.7 1.2 fusion.98
  180.9 1.2 fusion.98
  182.2 1.2 fusion.98
  183.4 1.2 fusion.98
  184.6 1.2 fusion.98
  185.8 1.2 fusion.98
  187.0 1.2 fusion.98
  188.3 1.2 fusion.98
  190.7 1.2 fusion.98
  191.9 1.2 fusion.98
  195.6 1.2 fusion.98
  196.8 1.2 fusion.98
  200.4 1.2 fusion.98
  201.7 1.2 fusion.98
  205.3 1.2 fusion.98
  209.0 1.2 fusion.98
  210.2 1.2 fusion.98
  213.8 1.2 fusion.98
  215.0 1.2 fusion.98
  218.7 1.2 fusion.98
  219.9 1.2 fusion.98
  223.6 1.2 fusion.98
  224.8 1.2 fusion.98
  228.4 1.2 fusion.98
  232.1 1.2 fusion.98
  233.3 1.2 fusion.98
  237.0 1.2 fusion.98
  238.2 1.2 fusion.98
  241.8 1.2 fusion.98
  243.1 1.2 fusion.98
  245.7 2.8 multiply_reduce_fusion
  250.4 1.3 fusion.13
  252.6 1.6 gather_fusion
  255.4 2.9 fusion.46
  259.2 1.6 fusion.70
  260.9 2.3 fusion.22
  263.9 3.8 fusion.69
  267.8 6.2 fusion.37
  274.0 34.1 %all-reduce.3.cloned.1.call-done = f32[128,1024]{1,0:T(8,128)} async-done(((f32[128,1024]{1,0:T(8,128)}), f32[128,1024]{1,0:T(8,128)}) %all-reduce.3.cloned.1.call-update) | async-done | bytes 524304 | tf_op jit(solution)/shard_map/psum | solution.py:75
  308.1 1.2 add_convert_fusion.1
  309.4 2.8 gather_fusion.1
  312.2 2.6 add_convert_fusion
  314.7 141.7 %reduce-scatter.5.cloned.1.call-done = f32[16,1024]{1,0:T(8,128)} async-done(((f32[1024,1024]{1,0:T(8,128)}), f32[16,1024]{1,0:T(8,128)}) %reduce-scatter.5.cloned.1.call-update) | async-done | bytes 65552 | tf_op jit(solution)/shard_map/reduce_scatter | solution.py:92
  456.4 155.1 %reduce-scatter.3.cloned.1.call-done = f32[32,1024]{1,0:T(8,128)} async-done(((f32[2048,1024]{1,0:T(8,128)}), f32[32,1024]{1,0:T(8,128)}) %reduce-scatter.3.cloned.1.call-update) | async-done | bytes 131088 | tf_op jit(solution)/shard_map/reduce_scatter | solution.py:91
  (152 shorter events, 39.3 us)
Async XLA Ops:
  7.2 252.0 %copy-start = (bf16[1024,1024]{1,0:T(8,128)(2,1)S(1)}, bf16[1024,1024]{1,0:T(8,128)(2,1)}, u32[]{:S(2)}) copy-start(bf16[1024,1024]{1,0:T(8,128)(2,1)} %param.30) | copy-start | bytes 6291460
  7.2 5.3 copy-start.4
  7.2 3.4 copy-start.8
  7.2 3.4 copy-start.10
  7.2 160.3 %all-gather.4.cloned.1.call-start = ((), (), s32[]{:S(2)}) async-start(), calls=%async_computation.5 | async-start | bytes 34078720 | tf_op jit(solution)/shard_map/all_gather | solution.py:11
  21.0 3.6 copy-start.6
  21.0 7.6 %copy-start.9 = (bf16[1024]{0:T(1024)(128)(2,1)S(1)}, bf16[1024]{0:T(1024)(128)(2,1)}, u32[]{:S(2)}) copy-start(bf16[1024]{0:T(1024)(128)(2,1)} %param.28) | copy-start | bytes 6148
  24.6 283.6 %all-reduce.3.cloned.1.call-start = ((), (), s32[]{:S(2)}) async-start(), calls=%async_computation.2 | async-start | bytes 1048576 | tf_op jit(solution)/shard_map/psum | solution.py:75
  28.6 43.7 %copy-start.1 = (f32[512,1024]{0,1:T(8,128)S(1)}, f32[512,1024]{0,1:T(8,128)}, u32[]{:S(2)}) copy-start(f32[512,1024]{0,1:T(8,128)} %copy.28) | copy-start | bytes 6291460
  248.5 1.2 copy-start.5
  248.5 1.9 copy-start.11
  250.4 1.3 copy-start.7
  258.4 0.8 copy-start.2
  260.9 195.6 %reduce-scatter.5.cloned.1.call-start = ((), (), s32[]{:S(2)}) async-start(), calls=%async_computation.4 | async-start | bytes 4259840 | tf_op jit(solution)/shard_map/reduce_scatter | solution.py:92
  263.2 0.7 copy-start.3
  267.7 343.8 %reduce-scatter.3.cloned.1.call-start = ((), (), s32[]{:S(2)}) async-start(), calls=%async_computation.3 | async-start | bytes 8519680 | tf_op jit(solution)/shard_map/reduce_scatter | solution.py:91
Sparse Core Ops, SparseCore 0:
  24.7 142.8 all-gather.3
  261.0 47.1 all-reduce.2
  312.8 143.5 reduce-scatter.4
  461.7 149.8 reduce-scatter.2
where the time goes:
time: 623 us; the launch traced here: 618 us
  waiting for transfers between devices  407 us (65%)
  other arithmetic  84.4 us (14%)
  matrix products  54.4 us (9%)
  blocking collectives  41.2 us (7%)
  between operations  17 us (3%)
  local copies, waits for them, and re-layouts  12.1 us (2%)
    reduce_scatter x1, waiting for transfers between devices, weight_grads(): lax.psum_scatter(up_term, 'seq', scatter_dimension=0, tiled=True)  155 us
    reduce_scatter x1, waiting for transfers between devices, weight_grads(): lax.psum_scatter(down_term, 'seq', scatter_dimension=0, tiled=True)  142 us
    all_gather x1, waiting for transfers between devices, carried_in(): everything = jax.tree.map(lambda part: lax.all_gather(part, axis), x)  75.5 us
    select_n x64, other arithmetic, step(): return jax.tree.map(lambda a, b: jnp.where(reached, a, b), new, before)  75.2 us
    all_gather x1, blocking collectives, carried_in(): everything = jax.tree.map(lambda part: lax.all_gather(part, axis), x)  41.2 us
    psum x1, waiting for transfers between devices, inner_layer(): summed = lax.psum(partial_value, 'mlp')  34.1 us
    dot_general x1, matrix products, block_terms(): within = jnp.einsum('tsh,shp->thp', mixing, weighted, precision=HIGHEST)  19.6 us
  transfers between devices with their start and end apart: 4, of which 4 were waited for; matrix products, arithmetic and copies ran while one was open for 7% of the time, Pallas kernels for 0%

commit v1 on v0

v1 whole, which is shorter than its diff:
```python
import functools

import jax
import jax.numpy as jnp
from jax import lax
from jax.experimental import pallas as pl
from jax.experimental.pallas import tpu as pltpu
from jax.sharding import PartitionSpec as P

F32, BF16 = jnp.float32, jnp.bfloat16
HIGHEST = lax.Precision.HIGHEST
MESH = pl.DeviceIdType.MESH

ROWS = 512
D = 1024
HEADS = 16
HEAD = 64
NS = 128
Q = 128
CHUNKS = ROWS // Q
SLOTS = 128
XN, CN = 4, 2
PLANE = XN * CN
NQ = 4
W = D // NQ
PIECE = 272
EPS = 1e-05
G0, G1 = 0.7978845608028654, 0.044715


def nn(a, b):
    return jnp.dot(a, b, preferred_element_type=F32)


def nt(a, b):
    return lax.dot_general(a, b, (((1,), (1,)), ((), ())), preferred_element_type=F32)


def split3(x):
    hi = x.astype(BF16).astype(F32)
    mid = (x - hi).astype(BF16).astype(F32)
    return hi, mid, x - hi - mid


def in_rows(parts, shape):
    ids = lax.broadcasted_iota(jnp.int32, shape, 0)
    block = jnp.zeros(shape, F32)
    for i, part in enumerate(parts):
        block = jnp.where(ids == i, part, block)
    return block


def kernel(
    zn, yn,
    tokens, positions, value_proj, write_proj, read_proj, step_proj, step_bias, decay_rate, reset_depth,
    out_proj, router, pad_vector, up_weight, down_weight, cotangent,
    mixed, up_out, down_out,
    tok, pos, vp, wr, sp, bias, rate, reset, op, rout, pad, up, down, cot,
    normed, kr, vals, zrow, zcol, expander, dtv, ece, state, chunk_state, dpre, within,
    p1s, p1r, p2s, p2r, p3s, incoming,
    encoded, groups, select, mct, padup, pad_col, padsq,
    xn, gg, scale, slope, fac, turned, lt, lto, vx, vr,
    partial, ars, ar1, io,
    own, prod, ra1, rb1, ra_left, ra_right, rb_left, rb_right, total, zs, zd, zu, zv,
    load, ss, rs,
):
    sn = zn * PLANE
    ru, rd = 2 * D // sn, D // sn
    zh = zn // 2
    qw = D // yn
    seq, y = lax.axis_index("seq"), lax.axis_index("mlp")
    z, me = seq // PLANE, lax.rem(seq, PLANE)
    x, core = me // CN, lax.rem(me, CN)

    def plane_at(j):
        return z * PLANE + j

    pairs = [
        (tokens, tok), (write_proj, wr.at[:, 0:NS]), (read_proj, wr.at[:, NS : 2 * NS]), (step_proj, sp),
        (step_bias, bias), (decay_rate, rate), (reset_depth, reset), (value_proj, vp), (positions, pos),
        (pad_vector, pad), (out_proj, op), (router, rout), (up_weight, up), (cotangent, cot), (down_weight, down),
    ]
    loads = [pltpu.make_async_copy(a, b, load.at[i]) for i, (a, b) in enumerate(pairs)]
    for copy in loads:
        copy.start()

    barrier = pltpu.get_barrier_semaphore()
    peers = 0
    for oy in range(yn):
        for o in range(PLANE):
            if o or oy:
                peers += 1
                pl.semaphore_signal(
                    barrier, inc=1, device_id_type=MESH,
                    device_id=(plane_at(lax.rem(me + o, PLANE)), lax.rem(y + oy, yn)),
                )
    for o in range(1, zn):
        peers += 1
        pl.semaphore_signal(
            barrier, inc=1, device_id_type=MESH, device_id=(lax.rem(z + o, zn) * PLANE + me, y)
        )

    count = [0]

    def ids(n):
        count[0] += n
        return count[0] - n

    def rdma(src, dst, i, to_seq, to_y):
        return pltpu.make_async_remote_copy(
            src_ref=src, dst_ref=dst, send_sem=ss.at[i], recv_sem=rs.at[i],
            device_id=(to_seq, to_y), device_id_type=MESH,
        )

    for copy in loads[:7]:
        copy.wait()

    def norm(b, carry):
        rows = pl.ds(pl.multiple_of(b * Q, Q), Q)
        field = tok[rows, :].astype(F32)
        ms = jnp.mean(field * field, axis=-1, keepdims=True)
        normed[rows, :] = (field * lax.rsqrt(ms + EPS)).astype(BF16)
        return carry

    lax.fori_loop(0, CHUNKS, norm, 0)
    e_row = lax.rem(lax.broadcasted_iota(jnp.int32, (2 * Q, D), 0), HEADS)
    e_col = lax.broadcasted_iota(jnp.int32, (2 * Q, D), 1) // HEAD
    expander[...] = (e_row == e_col).astype(F32).astype(BF16)

    eye = lax.broadcasted_iota(jnp.int32, (HEADS, HEADS), 0) == lax.broadcasted_iota(jnp.int32, (HEADS, HEADS), 1)

    def column(row):
        return jnp.sum(jnp.where(eye, jnp.broadcast_to(row, (HEADS, HEADS)), 0.0), axis=1, keepdims=True)

    kr[...] = nn(normed[...], wr[...]).astype(BF16)
    step_t = sp[...].astype(F32).T.astype(BF16)
    raw = nt(step_t, normed[...]) + column(bias[...])
    dt_all = jnp.maximum(raw, 0.0) + jnp.log1p(jnp.exp(-jnp.abs(raw)))
    ld_all = -dt_all * column(rate[...]) - reset[...]
    s_id = lax.broadcasted_iota(jnp.int32, (Q, Q), 0)
    t_id = lax.broadcasted_iota(jnp.int32, (Q, Q), 1)
    before = (s_id <= t_id).astype(F32)
    for c in range(CHUNKS):
        cols = slice(c * Q, (c + 1) * Q)
        dt = dt_all[:, cols]
        cum = jnp.dot(ld_all[:, cols], before, precision=HIGHEST, preferred_element_type=F32)
        tail = jnp.exp(cum[:, Q - 1 : Q] - cum) * dt
        block = jnp.concatenate([dt, cum, tail, jnp.exp(cum), jnp.zeros((64, Q), F32)], axis=0)
        zrow[c] = block
        zcol[c] = block.T
    loads[7].wait()

    def values(b, carry):
        rows = pl.ds(pl.multiple_of(b * 256, 256), 256)
        vals[rows, :] = nn(normed[rows, :], vp[...]).astype(BF16)
        return carry

    lax.fori_loop(0, ROWS // 256, values, 0)

    state[...] = jnp.zeros_like(state)

    def chunk(c, decay):
        rows = pl.ds(pl.multiple_of(c * Q, Q), Q)
        zt = zcol[c]
        hi, mid, unused = split3(zt)
        kind = lax.broadcasted_iota(jnp.int32, (Q, Q), 1) // HEADS

        def expand(k):
            lhs = jnp.concatenate([jnp.where(kind == k, hi, 0.0), jnp.where(kind == k, mid, 0.0)], axis=1)
            return nn(lhs.astype(BF16), expander[...])

        v = vals[rows, :].astype(F32)
        dtv[rows, :] = (expand(0) * v).astype(BF16)
        weighted = (expand(2) * v).astype(BF16)
        grown = expand(3)
        ece[rows, :] = grown
        keys_t = kr[rows, 0:NS].astype(F32).T.astype(BF16)
        old = state[...]
        chunk_state[c] = old
        dpre[c] = jnp.broadcast_to(decay, (8, D))
        last = grown[Q - 1 : Q, :]
        state[...] = last * old + nn(keys_t, weighted)
        return decay * last

    decay = lax.fori_loop(0, CHUNKS, chunk, jnp.ones((1, D), F32))

    dpre[CHUNKS] = jnp.broadcast_to(decay, (8, D))
    mine = pl.ds(pl.multiple_of(y * qw, qw), qw)
    decay_rows = in_rows(split3(dpre[CHUNKS, 0:1, mine]), (16, qw)).astype(BF16)
    for j in range(PLANE):
        p1s[j, 0:16, :] = state[16 * j : 16 * j + 16, mine].astype(BF16)
        p1s[j, 16:32, :] = decay_rows
    p1r[0] = p1s[me]
    pl.semaphore_wait(barrier, peers)
    base = ids(PLANE)
    step1 = []
    for o in range(1, PLANE):
        j = lax.rem(me + o, PLANE)
        step1.append(rdma(p1s.at[j], p1r.at[o], base + o, plane_at(j), y))
        step1[-1].start()

    def intra(c, carry):
        rows = pl.ds(pl.multiple_of(c * Q, Q), Q)
        scores = nt(kr[rows, NS : 2 * NS], kr[rows, 0:NS])
        scores = jnp.where(s_id >= t_id, scores, 0.0)
        first = lax.broadcasted_iota(jnp.int32, (Q, 2 * HEAD), 1) < HEAD
        zr, zt = zrow[c], zcol[c]
        for pair in range(HEADS // 2):
            lanes = slice(2 * HEAD * pair, 2 * HEAD * (pair + 1))
            both = dtv[rows, lanes].astype(F32)
            right = jnp.concatenate([jnp.where(first, both, 0.0), jnp.where(first, 0.0, both)], axis=0)
            mixing = []
            for h in (2 * pair, 2 * pair + 1):
                gap = zt[:, HEADS + h : HEADS + h + 1] - zr[HEADS + h : HEADS + h + 1, :]
                mixing.append(scores * jnp.exp(jnp.minimum(gap, 0.0)))
            within[rows, lanes] = nn(jnp.concatenate(mixing, axis=1).astype(BF16), right.astype(BF16))
        return carry

    lax.fori_loop(0, CHUNKS // 2, intra, 0)

    def read(block):
        block = block.astype(F32)
        return block[0:16], block[16:17] + block[17:18] + block[18:19]

    for copy in step1:
        copy.wait_recv()
    pre, pre_decay = [jnp.zeros((16, qw), F32)], [jnp.ones((1, qw), F32)]
    for k in range(PLANE):
        new, by = read(p1r[lax.rem(me - k + PLANE, PLANE)])
        pre.append(by * pre[-1] + new)
        pre_decay.append(by * pre_decay[-1])
    p2s[0:16, :] = pre[-1].astype(BF16)
    p2s[16:32, :] = in_rows(split3(pre_decay[-1]), (16, qw)).astype(BF16)
    p2r[0] = p2s[...]
    base = ids(zn)
    step2 = [None]
    for o in range(1, zn):
        step2.append(rdma(p2s, p2r.at[o], base + o, lax.rem(z + o, zn) * PLANE + me, y))
        pl.when(z + o < zn)(step2[o].start)

    lax.fori_loop(CHUNKS // 2, CHUNKS, intra, 0)

    for o in range(1, zn):
        pl.when(z >= o)(step2[o].wait_recv)
    start = jnp.zeros((16, qw), F32)
    for k in range(zn - 1):
        new, by = read(p2r[jnp.maximum(z - k, 0)])
        start = jnp.where(k < z, by * start + new, start)
    for k in range(PLANE):
        p3s[k] = (pre_decay[k] * start + pre[k]).astype(BF16)

    def landing(j, at_y):
        return incoming.at[pl.ds(pl.multiple_of(j * 16, 16), 16), pl.ds(pl.multiple_of(at_y * qw, qw), qw)]

    base = ids(PLANE * yn)
    step3, from3 = [], []
    for o in range(PLANE):
        for oy in range(yn):
            if o or oy:
                i = base + o * yn + oy
                j, at_y = lax.rem(me + o, PLANE), lax.rem(y + oy, yn)
                step3.append(rdma(p3s.at[j], landing(me, y), i, plane_at(j), at_y))
                step3[-1].start()
                j, at_y = lax.rem(me - o + PLANE, PLANE), lax.rem(y - oy + yn, yn)
                from3.append(rdma(p3s.at[j], landing(j, at_y), i, plane_at(j), at_y))
    incoming[pl.ds(pl.multiple_of(me * 16, 16), 16), mine] = p3s[me]

    for copy in loads[8:]:
        copy.wait()
    local = pos[...] - seq * ROWS
    n_pos = local.shape[1]
    high, low = local >> 7, local & 127
    ids8 = lax.broadcasted_iota(jnp.int32, (8, n_pos), 0)
    left = jnp.where((jnp.broadcast_to(high, (8, n_pos)) == ids8) & (ids8 < CHUNKS), 1.0, 0.0).astype(BF16)
    ids128 = lax.broadcasted_iota(jnp.int32, (Q, n_pos), 0)
    right = jnp.where(jnp.broadcast_to(low, (Q, n_pos)) == ids128, 1.0, 0.0).astype(BF16)
    marks = nt(left, right)
    running = nn(marks.astype(BF16), before.astype(BF16))
    parts, so_far = [], jnp.zeros((1, 1), F32)
    for c in range(CHUNKS):
        parts.append(running[c : c + 1] + so_far)
        so_far = parts[-1][:, Q - 1 : Q]
    group_of = jnp.concatenate(parts, axis=1) - 1.0
    mark = jnp.concatenate([marks[c : c + 1] for c in range(CHUNKS)], axis=1)
    slot = lax.broadcasted_iota(jnp.int32, (SLOTS, ROWS), 0).astype(F32)
    member = jnp.where(slot == group_of, 1.0, 0.0)
    select[...] = (member * mark).astype(BF16)
    pad_row = pad[...].astype(F32)
    padsq[...] = jnp.broadcast_to(jnp.sum(pad_row * pad_row, axis=-1, keepdims=True), (8, 128))
    pad_col[...] = jnp.broadcast_to(pad_row, (128, D)).T
    padup[...] = nn(jnp.broadcast_to(pad_row, (16, D)).astype(BF16), up[D : 2 * D, :])

    for copy in from3:
        copy.wait_recv()

    def encode(b, carry):
        for k in range(2):
            c = 2 * b + k
            rows = pl.ds(pl.multiple_of(c * Q, Q), Q)
            full = chunk_state[c] + dpre[c, 0:1, :] * incoming[...].astype(F32)
            carried = nn(kr[rows, NS : 2 * NS], full.astype(BF16))
            scanned = within[rows, :] + ece[rows, :] * carried
            ms = jnp.mean(scanned * scanned, axis=-1, keepdims=True)
            normed[rows, :] = (scanned * lax.rsqrt(ms + EPS)).astype(BF16)
        rows = pl.ds(pl.multiple_of(b * 256, 256), 256)
        encoded[rows, :] = (tok[rows, :].astype(F32) + nn(normed[rows, :], op[...])).astype(BF16)
        return carry

    lax.fori_loop(0, 2, encode, 0)
    logits = nt(in_rows(split3(rout[...]), (16, D)).astype(BF16), encoded[...])
    confidence = 1.0 / (1.0 + jnp.exp(-jnp.sum(logits, axis=0, keepdims=True)))
    weight = member * confidence
    weight_hi = weight.astype(BF16)
    weight_lo = (weight - weight_hi.astype(F32)).astype(BF16)
    mct[:, 0:SLOTS] = weight_hi.astype(F32).T.astype(BF16)
    mct[:, SLOTS : 2 * SLOTS] = weight_lo.astype(F32).T.astype(BF16)
    groups[...] = nn(select[...], encoded[...])
    grads = nn(weight_hi, cot[...]) + nn(weight_lo, cot[...])
    gg[...] = grads.astype(BF16)
    rows_f = groups[...]
    ms = (jnp.sum(rows_f * rows_f, axis=-1, keepdims=True) + padsq[0:1, 0:1]) * (0.5 / D)
    r = lax.rsqrt(ms + EPS)
    scale[...] = jnp.broadcast_to(r, (SLOTS, 128))
    inner = rows_f * r
    xn[...] = inner.astype(BF16)

    def turn(field, first_row, each, blocks):
        turned[...] = field.T.astype(BF16)
        for k in range(XN):
            at = lax.rem(x + k, XN)
            for b in range(blocks):
                rows = slice(first_row + b * each, first_row + (b + 1) * each)
                begin = (b * PLANE + at * CN + core) * each
                lt[k, rows, 0:SLOTS] = turned[pl.ds(pl.multiple_of(begin, 16), each), :]
                begin = (b * PLANE + at * CN + 1 - core) * each
                lto[k, rows, :] = turned[pl.ds(pl.multiple_of(begin, 16), each), :]

    turn(inner, 0, ru, zh)
    turn(grads, 128, rd, zn)
    mate = plane_at(x * CN + 1 - core)
    base = ids(4)
    swaps = [
        rdma(lto, lt.at[:, :, SLOTS : 2 * SLOTS], base, mate, y),
        rdma(fac.at[1, 0:SLOTS, :], fac.at[1, SLOTS : 2 * SLOTS, :], base + 1, mate, y),
        rdma(fac.at[0, 0:SLOTS, :], fac.at[0, SLOTS : 2 * SLOTS, :], base + 2, mate, y),
        rdma(vx, vr, base + 3, mate, y),
    ]
    swaps[0].start()

    def forward(b, carry):
        cols = pl.ds(pl.multiple_of(b * 256, 256), 256)
        pre_act = nn(xn[...], up[0:D, cols]) + scale[:, 0:1] * padup[0:1, cols]
        square = pre_act * pre_act
        bend = jnp.tanh(G0 * pre_act * (1.0 + G1 * square))
        fac[1, 0:SLOTS, cols] = (0.5 * pre_act * (1.0 + bend)).astype(BF16)
        slope[:, cols] = 0.5 * (1.0 + bend) + 0.5 * pre_act * (1.0 - bend * bend) * (
            G0 * (1.0 + 3.0 * G1 * square)
        )
        return carry

    lax.fori_loop(0, 4, forward, 0)
    swaps[1].start()

    def backward(b, carry):
        cols = pl.ds(pl.multiple_of(b * 256, 256), 256)
        pre_grad = (nn(gg[...], down[:, cols]) * slope[:, cols]).astype(BF16)
        fac[0, 0:SLOTS, cols] = pre_grad
        pad_term = jnp.sum(pre_grad.astype(F32) * scale[:, 0:1], axis=0, keepdims=True)
        vx[:, cols] = jnp.broadcast_to(pad_term, (8, 256))
        return carry

    lax.fori_loop(0, 4, backward, 0)
    swaps[2].start()
    swaps[3].start()

    rq = SLOTS // yn
    partial[...] = nt(fac[1, 0:SLOTS, :], down[...])
    ars[...] = partial[...].astype(BF16)
    base = ids(2 * yn)
    share1, share2, from2 = [], [], []
    my_rows = pl.ds(pl.multiple_of(y * rq, rq), rq)
    for o in range(1, yn):
        at_y = lax.rem(y + o, yn)
        share1.append(rdma(ars.at[pl.ds(pl.multiple_of(at_y * rq, rq), rq), :], ar1.at[o - 1], base + o, seq, at_y))
        share1[-1].start()
        share2.append(rdma(io.at[my_rows, :], io.at[my_rows, :], base + yn + o, seq, at_y))
        at_y = lax.rem(y - o + yn, yn)
        other = pl.ds(pl.multiple_of(at_y * rq, rq), rq)
        from2.append(rdma(io.at[other, :], io.at[other, :], base + yn + o, seq, at_y))

    for copy in swaps:
        copy.wait_recv()
    right_x = plane_at(lax.rem(x + 1, XN) * CN + core)
    left_x = plane_at(lax.rem(x + XN - 1, XN) * CN + core)
    upper, lower = slice(0, 128), slice(128, PIECE)
    ahead, later, along = [], [], []

    def multiply(q):
        cols = slice(q * W, (q + 1) * W)
        pad_rows = in_rows([vx[0:1, cols] + vr[0:1, cols]], (16, W))
        own[q, 256:PIECE, :] = pad_rows
        for k in range(1, XN):
            prod[k, q, 256:PIECE, :] = pad_rows.astype(BF16)
        for part in range(2):
            rows = slice(128 * part, 128 * part + 128)
            for k in (2, 1, 3, 0):
                term = nn(lt[k, rows, :], fac[part, :, cols])
                if k:
                    prod[k, q, rows, :] = term.astype(BF16)
                else:
                    own[q, rows, :] = term

    def send_ahead(q):
        base = ids(4)
        ahead.append([
            rdma(prod.at[2, q, upper, :], ra1.at[q], base, right_x, y),
            rdma(prod.at[2, q, lower, :], rb1.at[q], base + 1, left_x, y),
            rdma(prod.at[1, q, lower, :], rb_left.at[q], base + 2, right_x, y),
            rdma(prod.at[3, q, upper, :], ra_right.at[q], base + 3, left_x, y),
        ])
        for copy in ahead[q]:
            copy.start()

    def send_later(q):
        base = ids(2)
        later.append([
            rdma(prod.at[1, q, upper, :], ra_left.at[q], base, right_x, y),
            rdma(prod.at[3, q, lower, :], rb_right.at[q], base + 1, left_x, y),
        ])
        ahead[q][0].wait_recv()
        prod[1, q, upper, :] = (prod[1, q, upper, :].astype(F32) + ra1[q].astype(F32)).astype(BF16)
        later[q][0].start()
        ahead[q][1].wait_recv()
        prod[3, q, lower, :] = (prod[3, q, lower, :].astype(F32) + rb1[q].astype(F32)).astype(BF16)
        later[q][1].start()

    def send_along(q):
        for copy in ahead[q][2:] + later[q]:
            copy.wait_recv()
        a = own[q, upper, :] + ra_left[q].astype(F32) + ra_right[q].astype(F32)
        b = own[q, lower, :] + rb_left[q].astype(F32) + rb_right[q].astype(F32)
        total[q, upper, :] = a
        total[q, lower, :] = b
        zs[q, upper, :] = a.astype(BF16)
        zs[q, lower, :] = b.astype(BF16)
        base = ids(2 * zn)
        for o in range(1, zn):
            to = lax.rem(z + o, zn)
            dev = to * PLANE + me
            up_rows = pl.ds(pl.multiple_of(ru * jnp.minimum(to, zh - 1), 16), ru)
            down_rows = pl.ds(pl.multiple_of(128 + rd * to, 16), rd)
            c_down = rdma(zs.at[q, down_rows, :], zd.at[q, o - 1], base + o, dev, y)
            c_up = rdma(zs.at[q, up_rows, :], zu.at[q, o - 1], base + zn + o, dev, y)
            c_pad = rdma(zs.at[q, 256:PIECE, :], zv.at[q, o - 1], base + zn + o, dev, y)
            pl.when(to < zh)(c_up.start)
            pl.when(to >= zh)(c_pad.start)
            c_down.start()
            along.append((q, to, c_down, c_up, c_pad))

    def reduce_share():
        for copy in share1:
            copy.wait_recv()
        summed = groups[my_rows, :] + partial[my_rows, :]
        for o in range(1, yn):
            summed = summed + ar1[o - 1].astype(F32)
        io[my_rows, :] = summed.astype(BF16)
        for copy in share2:
            copy.start()

    def mix():
        for copy in from2:
            copy.wait_recv()

        def some(c, carry):
            rows = pl.ds(pl.multiple_of(c * Q, Q), Q)
            both = io[...]
            spread = nn(mct[rows, :], jnp.concatenate([both, both], axis=0))
            mixed[rows, :] = (encoded[rows, :].astype(F32) + spread).astype(BF16)
            return carry

        lax.fori_loop(0, CHUNKS, some, 0)

    multiply(0)
    send_ahead(0)
    multiply(1)
    send_ahead(1)
    reduce_share()
    send_later(0)
    for q in range(2, NQ):
        multiply(q)
        send_ahead(q)
        send_later(q - 1)
        if q == 2:
            mix()
        send_along(q - 2)
    send_later(NQ - 1)
    send_along(NQ - 2)
    send_along(NQ - 1)

    pad_part = pad_col[pl.ds(pl.multiple_of(ru * jnp.maximum(seq - sn // 2, 0), 16), ru), 0:1]
    for q in range(NQ):
        cols = slice(q * W, (q + 1) * W)
        for at, to, c_down, c_up, c_pad in along:
            if at == q:
                c_down.wait_recv()
                pl.when(z < zh)(c_up.wait_recv)
                pl.when(z >= zh)(c_pad.wait_recv)
        down_sum = total[q, pl.ds(pl.multiple_of(128 + rd * z, 16), rd), :]
        for o in range(zn - 1):
            down_sum = down_sum + zd[q, o].astype(F32)
        down_out[:, cols] = down_sum

        @pl.when(z < zh)
        def _():
            up_sum = total[q, pl.ds(pl.multiple_of(ru * jnp.minimum(z, zh - 1), 16), ru), :]
            for o in range(zn - 1):
                up_sum = up_sum + zu[q, o].astype(F32)
            up_out[:, cols] = up_sum

        @pl.when(z >= zh)
        def _():
            pad_sum = total[q, 256:257, :]
            for o in range(zn - 1):
                pad_sum = pad_sum + zv[q, o, 0:1, :].astype(F32)
            up_out[:, cols] = pad_part * pad_sum

    for copy in step1 + step3 + swaps + share1 + share2:
        copy.wait_send()
    for o in range(1, zn):
        pl.when(z + o < zn)(step2[o].wait_send)
    for q in range(NQ):
        for copy in ahead[q] + later[q]:
            copy.wait_send()
    for q, to, c_down, c_up, c_pad in along:
        c_down.wait_send()
        pl.when(to < zh)(c_up.wait_send)
        pl.when(to >= zh)(c_pad.wait_send)


def on_device(
    zn, yn, tokens, positions, value_proj, write_proj, read_proj, step_proj, step_bias, decay_rate, reset_depth,
    out_proj, router, pad_vector, up_weight, down_weight, cotangent,
):
    sn = zn * PLANE
    ru, rd, qw = 2 * D // sn, D // sn, D // yn
    n_pos = positions.shape[0]
    vm = pltpu.VMEM
    n_sem = PLANE + zn + PLANE * yn + 4 + 2 * yn + NQ * (6 + 2 * zn)
    scratch = [
        vm((ROWS, D), BF16), vm((1, n_pos), jnp.int32), vm((D, D), BF16), vm((D, 2 * NS), BF16), vm((D, HEADS), BF16),
        vm((1, HEADS), F32), vm((1, HEADS), F32), vm((1, ROWS), F32), vm((D, D), BF16), vm((1, D), F32),
        vm((1, D), BF16), vm((2 * D, D), BF16), vm((D, D), BF16), vm((ROWS, D), BF16),
        vm((ROWS, D), BF16), vm((ROWS, 2 * NS), BF16), vm((ROWS, D), BF16), vm((CHUNKS, Q, Q), F32),
        vm((CHUNKS, Q, Q), F32), vm((2 * Q, D), BF16), vm((ROWS, D), BF16), vm((ROWS, D), F32), vm((NS, D), F32),
        vm((CHUNKS, NS, D), F32), vm((CHUNKS + 1, 8, D), F32), vm((ROWS, D), F32),
        vm((PLANE, 32, qw), BF16), vm((PLANE, 32, qw), BF16), vm((32, qw), BF16), vm((zn, 32, qw), BF16),
        vm((PLANE, 16, qw), BF16), vm((NS, D), BF16),
        vm((ROWS, D), BF16), vm((SLOTS, D), F32), vm((SLOTS, ROWS), BF16), vm((ROWS, 2 * SLOTS), BF16),
        vm((16, D), F32), vm((D, 128), F32), vm((8, 128), F32),
        vm((SLOTS, D), BF16), vm((SLOTS, D), BF16), vm((SLOTS, 128), F32), vm((SLOTS, D), F32),
        vm((2, 2 * SLOTS, D), BF16), vm((D, SLOTS), BF16), vm((XN, 256, 2 * SLOTS), BF16), vm((XN, 256, SLOTS), BF16),
        vm((8, D), F32), vm((8, D), F32),
        vm((SLOTS, D), F32), vm((SLOTS, D), BF16), vm((max(yn - 1, 1), SLOTS // yn, D), BF16), vm((SLOTS, D), BF16),
        vm((NQ, PIECE, W), F32), vm((XN, NQ, PIECE, W), BF16), vm((NQ, 128, W), BF16), vm((NQ, 144, W), BF16),
        vm((NQ, 128, W), BF16), vm((NQ, 128, W), BF16), vm((NQ, 144, W), BF16), vm((NQ, 144, W), BF16),
        vm((NQ, PIECE, W), F32), vm((NQ, PIECE, W), BF16), vm((NQ, zn - 1, rd, W), BF16), vm((NQ, zn - 1, ru, W), BF16),
        vm((NQ, zn - 1, 16, W), BF16),
        pltpu.SemaphoreType.DMA((15,)), pltpu.SemaphoreType.DMA((n_sem,)), pltpu.SemaphoreType.DMA((n_sem,)),
    ]
    return pl.pallas_call(
        functools.partial(kernel, zn, yn),
        out_shape=(
            jax.ShapeDtypeStruct((ROWS, D), BF16),
            jax.ShapeDtypeStruct((ru, D), F32),
            jax.ShapeDtypeStruct((rd, D), F32),
        ),
        in_specs=[pl.BlockSpec(memory_space=pl.ANY)] * 15,
        out_specs=(pl.BlockSpec(memory_space=pltpu.VMEM),) * 3,
        scratch_shapes=scratch,
        compiler_params=pltpu.CompilerParams(
            collective_id=0, has_side_effects=True, vmem_limit_bytes=60 * 2**20
        ),
    )(
        tokens, positions.reshape(1, n_pos), value_proj, write_proj, read_proj, step_proj, step_bias.reshape(1, HEADS),
        decay_rate.reshape(1, HEADS), reset_depth.reshape(1, ROWS), out_proj, router.reshape(1, D),
        pad_vector.reshape(1, D), up_weight, down_weight, cotangent,
    )


def solution(mesh):
    placed = (
        P("seq", None), P(), P(), P(), P(), P(), P(), P(), P("seq"), P(), P(), P(),
        P(None, "mlp"), P(None, "mlp"), P("seq", None),
    )
    return jax.shard_map(
        functools.partial(on_device, mesh.shape["seq"] // PLANE, mesh.shape["mlp"]),
        mesh=mesh,
        in_specs=placed,
        out_specs=(P("seq", None), P("seq", "mlp"), P("seq", "mlp")),
        check_vma=False,
    )
```

time: 623 us -> 75.3 us (0.12)
  waiting for transfers between devices: 407 us -> 0 us
  other arithmetic: 84.4 us -> 0 us
  Pallas kernels: 0 us -> 68 us
  matrix products: 54.4 us -> 0 us
  blocking collectives: 41.2 us -> 0 us
  between operations: 17 us -> 0.66 us
    reduce_scatter x2 -> x0, waiting for transfers between devices: 297 us -> none  [the longest x1 155 us: weight_grads(): lax.psum_scatter(up_term, 'seq', scatter_dimension=0, tiled=True)]
    select_n x67 -> x0, other arithmetic: 76.4 us -> none  [the longest x64 75.2 us: step(): return jax.tree.map(lambda a, b: jnp.where(reached, a, b), new, before)]
    all_gather x1 -> x0, waiting for transfers between devices: 75.5 us -> none  [carried_in(): everything = jax.tree.map(lambda part: lax.all_gather(part, axis), x)]
    pallas_call x0 -> x1, Pallas kernels: none -> 68 us  [on_device(): pl.pallas_call(functools.partial(kernel, zn, yn), out_shape=(jax.ShapeDty...]
    dot_general x15 -> x0, matrix products: 54.4 us -> none  [the longest x1 19.6 us: block_terms(): within = jnp.einsum('tsh,shp->thp', mixing, weighted, precision=HIGHEST)]
    all_gather x1 -> x0, blocking collectives: 41.2 us -> none  [carried_in(): everything = jax.tree.map(lambda part: lax.all_gather(part, axis), x)]
    psum x1 -> x0, waiting for transfers between devices: 34.1 us -> none  [inner_layer(): summed = lax.psum(partial_value, 'mlp')]
  transfers between devices with their start and end apart: 4 -> 0, of which waited for: 4 -> 0; matrix products, arithmetic and copies ran while one was open for 7% -> 0% of each run, Pallas kernels for 0% -> 0%
where the time goes in v1:
time: 75.3 us; the launch traced here: 75.1 us
  Pallas kernels  68 us (90%)
  local copies, waits for them, and re-layouts  6.47 us (9%)
    pallas_call x1, Pallas kernels, on_device(): pl.pallas_call(functools.partial(kernel, zn, yn), out_shape=(jax.ShapeDty...  68 us
    unnamed x8, local copies, waits for them, and re-layouts  5.19 us

profile of v1, /device:TPU:32, one launch (start us, length us, event | category | flops | bytes accessed | tf_op | source)
XLA Modules:
  0.0 75.1 jit_solution(7098388561487680428)
XLA Ops:
  0.6 1.3 %reshape.29.pad_vector = bf16[1,1024]{1,0:T(2,128)(2,1)} reshape(bf16[1024]{0:T(1024)(128)(2,1)} %param.26) | data formatting | bytes 4096 | tf_op jit(solution)/shard_map/reshape | solution.py:586
  1.9 1.6 %copy.18.step_proj = bf16[1024,16]{1,0:T(8,128)(2,1)} copy(bf16[1024,16]{0,1:T(8,128)(2,1)} %param.20) | data formatting | bytes 65536 | tf_op args[5]
  3.5 68.0 %shard_map.166 = (bf16[512,1024]{1,0:T(8,128)(2,1)}, f32[32,1024]{1,0:T(8,128)}, f32[16,1024]{1,0:T(8,128)}) custom-call(bf16[512,1024]{1,0:T(8,128)(2,1)} %tokens.1, s32[1,4096]{1,0:T(1,128)} %bitcast.5, bf16[1024,1024]{1,0:T(8,128)(2,1)} %value_proj.1, bf16[1024,128]{1,0:T(8,128)(2,1)} %write_proj.1, bf16[1024,128]{1,0:T(8,128)(2,1)} %read_proj.1, ...), custom_call_target="tpu_custom_call" | custom-call | tf_op jit(solution)/shard_map/pallas_call | solution.py:570
  71.5 0.0 copy-start
  71.5 0.0 copy-start.1
  71.5 2.3 %copy.22 = bf16[512,1024]{1,0:T(8,128)(2,1)} copy(bf16[512,1024]{1,0:T(8,128)(2,1)} %get-tuple-element.6) | data formatting | bytes 2097152
  73.8 0.0 copy-done
  73.8 0.7 copy.23
  74.5 0.0 copy-done.1
  74.5 0.6 copy.24
Async XLA Ops:
  71.5 2.3 %copy-start = (f32[32,1024]{1,0:T(8,128)S(1)}, f32[32,1024]{1,0:T(8,128)}, u32[]{:S(2)}) copy-start(f32[32,1024]{1,0:T(8,128)} %get-tuple-element.7) | copy-start | bytes 393220
  71.5 3.0 %copy-start.1 = (f32[16,1024]{1,0:T(8,128)S(1)}, f32[16,1024]{1,0:T(8,128)}, u32[]{:S(2)}) copy-start(f32[16,1024]{1,0:T(8,128)} %get-tuple-element.8) | copy-start | bytes 196612

commit v2 on v1

--- a/solution.py
+++ b/solution.py
@@ -54,7 +54,7 @@
     zn, yn,
     tokens, positions, value_proj, write_proj, read_proj, step_proj, step_bias, decay_rate, reset_depth,
     out_proj, router, pad_vector, up_weight, down_weight, cotangent,
-    mixed, up_out, down_out,
+    encoded_out, mct_out, io_out, up_out, down_out,
     tok, pos, vp, wr, sp, bias, rate, reset, op, rout, pad, up, down, cot,
     normed, kr, vals, zrow, zcol, expander, dtv, ece, state, chunk_state, dpre, within,
     p1s, p1r, p2s, p2r, p3s, incoming,
@@ -62,7 +62,7 @@
     xn, gg, scale, slope, fac, turned, lt, lto, vx, vr,
     partial, ars, ar1, io,
     own, prod, ra1, rb1, ra_left, ra_right, rb_left, rb_right, total, zs, zd, zu, zv,
-    load, ss, rs,
+    load, store, ss, rs,
 ):
     sn = zn * PLANE
     ru, rd = 2 * D // sn, D // sn
@@ -81,7 +81,7 @@
         (pad_vector, pad), (out_proj, op), (router, rout), (up_weight, up), (cotangent, cot), (down_weight, down),
     ]
     loads = [pltpu.make_async_copy(a, b, load.at[i]) for i, (a, b) in enumerate(pairs)]
-    for copy in loads:
+    for copy in loads[:8]:
         copy.start()
 
     barrier = pltpu.get_barrier_semaphore()
@@ -112,6 +112,9 @@
             device_id=(to_seq, to_y), device_id_type=MESH,
         )
 
+    step1, step2, step3, from3, swaps, share1, share2, from2 = [], [None], [], [], [], [], [], []
+    ahead, later, along = [], [], []
+
     for copy in loads[:7]:
         copy.wait()
 
@@ -133,8 +136,7 @@
         return jnp.sum(jnp.where(eye, jnp.broadcast_to(row, (HEADS, HEADS)), 0.0), axis=1, keepdims=True)
 
     kr[...] = nn(normed[...], wr[...]).astype(BF16)
-    step_t = sp[...].astype(F32).T.astype(BF16)
-    raw = nt(step_t, normed[...]) + column(bias[...])
+    raw = nt(sp[...], normed[...]) + column(bias[...])
     dt_all = jnp.maximum(raw, 0.0) + jnp.log1p(jnp.exp(-jnp.abs(raw)))
     ld_all = -dt_all * column(rate[...]) - reset[...]
     s_id = lax.broadcasted_iota(jnp.int32, (Q, Q), 0)
@@ -149,6 +151,8 @@
         zrow[c] = block
         zcol[c] = block.T
     loads[7].wait()
+    for copy in loads[8:]:
+        copy.start()
 
     def values(b, carry):
         rows = pl.ds(pl.multiple_of(b * 256, 256), 256)
@@ -193,7 +197,6 @@
     p1r[0] = p1s[me]
     pl.semaphore_wait(barrier, peers)
     base = ids(PLANE)
-    step1 = []
     for o in range(1, PLANE):
         j = lax.rem(me + o, PLANE)
         step1.append(rdma(p1s.at[j], p1r.at[o], base + o, plane_at(j), y))
@@ -233,7 +236,6 @@
     p2s[16:32, :] = in_rows(split3(pre_decay[-1]), (16, qw)).astype(BF16)
     p2r[0] = p2s[...]
     base = ids(zn)
-    step2 = [None]
     for o in range(1, zn):
         step2.append(rdma(p2s, p2r.at[o], base + o, lax.rem(z + o, zn) * PLANE + me, y))
         pl.when(z + o < zn)(step2[o].start)
@@ -253,7 +255,6 @@
         return incoming.at[pl.ds(pl.multiple_of(j * 16, 16), 16), pl.ds(pl.multiple_of(at_y * qw, qw), qw)]
 
     base = ids(PLANE * yn)
-    step3, from3 = [], []
     for o in range(PLANE):
         for oy in range(yn):
             if o or oy:
@@ -285,7 +286,8 @@
     slot = lax.broadcasted_iota(jnp.int32, (SLOTS, ROWS), 0).astype(F32)
     member = jnp.where(slot == group_of, 1.0, 0.0)
     select[...] = (member * mark).astype(BF16)
-    pad_row = pad[...].astype(F32)
+    pad_rows = pad[...].astype(F32)
+    pad_row = jnp.concatenate([pad_rows[i : i + 1] for i in range(8)], axis=1)
     padsq[...] = jnp.broadcast_to(jnp.sum(pad_row * pad_row, axis=-1, keepdims=True), (8, 128))
     pad_col[...] = jnp.broadcast_to(pad_row, (128, D)).T
     padup[...] = nn(jnp.broadcast_to(pad_row, (16, D)).astype(BF16), up[D : 2 * D, :])
@@ -314,6 +316,9 @@
     weight_lo = (weight - weight_hi.astype(F32)).astype(BF16)
     mct[:, 0:SLOTS] = weight_hi.astype(F32).T.astype(BF16)
     mct[:, SLOTS : 2 * SLOTS] = weight_lo.astype(F32).T.astype(BF16)
+    stores = [pltpu.make_async_copy(encoded, encoded_out, store.at[0]), pltpu.make_async_copy(mct, mct_out, store.at[1])]
+    for copy in stores:
+        copy.start()
     groups[...] = nn(select[...], encoded[...])
     grads = nn(weight_hi, cot[...]) + nn(weight_lo, cot[...])
     gg[...] = grads.astype(BF16)
@@ -339,7 +344,7 @@
     turn(grads, 128, rd, zn)
     mate = plane_at(x * CN + 1 - core)
     base = ids(4)
-    swaps = [
+    swaps += [
         rdma(lto, lt.at[:, :, SLOTS : 2 * SLOTS], base, mate, y),
         rdma(fac.at[1, 0:SLOTS, :], fac.at[1, SLOTS : 2 * SLOTS, :], base + 1, mate, y),
         rdma(fac.at[0, 0:SLOTS, :], fac.at[0, SLOTS : 2 * SLOTS, :], base + 2, mate, y),
@@ -377,7 +382,6 @@
     partial[...] = nt(fac[1, 0:SLOTS, :], down[...])
     ars[...] = partial[...].astype(BF16)
     base = ids(2 * yn)
-    share1, share2, from2 = [], [], []
     my_rows = pl.ds(pl.multiple_of(y * rq, rq), rq)
     for o in range(1, yn):
         at_y = lax.rem(y + o, yn)
@@ -393,8 +397,6 @@
     right_x = plane_at(lax.rem(x + 1, XN) * CN + core)
     left_x = plane_at(lax.rem(x + XN - 1, XN) * CN + core)
     upper, lower = slice(0, 128), slice(128, PIECE)
-    ahead, later, along = [], [], []
-
     def multiply(q):
         cols = slice(q * W, (q + 1) * W)
         pad_rows = in_rows([vx[0:1, cols] + vr[0:1, cols]], (16, W))
@@ -467,18 +469,11 @@
         for copy in share2:
             copy.start()
 
-    def mix():
+    def share():
         for copy in from2:
             copy.wait_recv()
-
-        def some(c, carry):
-            rows = pl.ds(pl.multiple_of(c * Q, Q), Q)
-            both = io[...]
-            spread = nn(mct[rows, :], jnp.concatenate([both, both], axis=0))
-            mixed[rows, :] = (encoded[rows, :].astype(F32) + spread).astype(BF16)
-            return carry
-
-        lax.fori_loop(0, CHUNKS, some, 0)
+        stores.append(pltpu.make_async_copy(io, io_out, store.at[2]))
+        stores[2].start()
 
     multiply(0)
     send_ahead(0)
@@ -491,7 +486,7 @@
         send_ahead(q)
         send_later(q - 1)
         if q == 2:
-            mix()
+            share()
         send_along(q - 2)
     send_later(NQ - 1)
     send_along(NQ - 2)
@@ -524,17 +519,27 @@
                 pad_sum = pad_sum + zv[q, o, 0:1, :].astype(F32)
             up_out[:, cols] = pad_part * pad_sum
 
+    for copy in stores:
+        copy.wait()
     for copy in step1 + step3 + swaps + share1 + share2:
         copy.wait_send()
-    for o in range(1, zn):
+    for o in range(1, len(step2)):
         pl.when(z + o < zn)(step2[o].wait_send)
-    for q in range(NQ):
-        for copy in ahead[q] + later[q]:
+    for copies in ahead + later:
+        for copy in copies:
             copy.wait_send()
     for q, to, c_down, c_up, c_pad in along:
         c_down.wait_send()
         pl.when(to < zh)(c_up.wait_send)
         pl.when(to >= zh)(c_pad.wait_send)
+
+
+def finish(encoded, mct, io, up_sum, down_sum, mixed, up_out, down_out):
+    both = io[...]
+    spread = nn(mct[...], jnp.concatenate([both, both], axis=0))
+    mixed[...] = (encoded[...].astype(F32) + spread).astype(BF16)
+    up_out[...] = up_sum[...]
+    down_out[...] = down_sum[...]
 
 
 def on_device(
@@ -547,9 +552,9 @@
     vm = pltpu.VMEM
     n_sem = PLANE + zn + PLANE * yn + 4 + 2 * yn + NQ * (6 + 2 * zn)
     scratch = [
-        vm((ROWS, D), BF16), vm((1, n_pos), jnp.int32), vm((D, D), BF16), vm((D, 2 * NS), BF16), vm((D, HEADS), BF16),
+        vm((ROWS, D), BF16), vm((1, n_pos), jnp.int32), vm((D, D), BF16), vm((D, 2 * NS), BF16), vm((HEADS, D), BF16),
         vm((1, HEADS), F32), vm((1, HEADS), F32), vm((1, ROWS), F32), vm((D, D), BF16), vm((1, D), F32),
-        vm((1, D), BF16), vm((2 * D, D), BF16), vm((D, D), BF16), vm((ROWS, D), BF16),
+        vm((8, D // 8), BF16), vm((2 * D, D), BF16), vm((D, D), BF16), vm((ROWS, D), BF16),
         vm((ROWS, D), BF16), vm((ROWS, 2 * NS), BF16), vm((ROWS, D), BF16), vm((CHUNKS, Q, Q), F32),
         vm((CHUNKS, Q, Q), F32), vm((2 * Q, D), BF16), vm((ROWS, D), BF16), vm((ROWS, D), F32), vm((NS, D), F32),
         vm((CHUNKS, NS, D), F32), vm((CHUNKS + 1, 8, D), F32), vm((ROWS, D), F32),
@@ -565,26 +570,51 @@
         vm((NQ, 128, W), BF16), vm((NQ, 128, W), BF16), vm((NQ, 144, W), BF16), vm((NQ, 144, W), BF16),
         vm((NQ, PIECE, W), F32), vm((NQ, PIECE, W), BF16), vm((NQ, zn - 1, rd, W), BF16), vm((NQ, zn - 1, ru, W), BF16),
         vm((NQ, zn - 1, 16, W), BF16),
-        pltpu.SemaphoreType.DMA((15,)), pltpu.SemaphoreType.DMA((n_sem,)), pltpu.SemaphoreType.DMA((n_sem,)),
+        pltpu.SemaphoreType.DMA((15,)), pltpu.SemaphoreType.DMA((3,)), pltpu.SemaphoreType.DMA((n_sem,)), pltpu.SemaphoreType.DMA((n_sem,)),
     ]
+    encoded, mct, io, up_sum, down_sum = pl.pallas_call(
+        functools.partial(kernel, zn, yn),
+        out_shape=(
+            jax.ShapeDtypeStruct((ROWS, D), BF16),
+            jax.ShapeDtypeStruct((ROWS, 2 * SLOTS), BF16),
+            jax.ShapeDtypeStruct((SLOTS, D), BF16),
+            jax.ShapeDtypeStruct((ru, D), F32),
+            jax.ShapeDtypeStruct((rd, D), F32),
+        ),
+        in_specs=[pl.BlockSpec(memory_space=pl.ANY)] * 15,
+        out_specs=(pl.BlockSpec(memory_space=pl.ANY),) * 3 + (pl.BlockSpec(memory_space=pltpu.VMEM),) * 2,
+        scratch_shapes=scratch,
+        compiler_params=pltpu.CompilerParams(
+            collective_id=0, has_side_effects=True, vmem_limit_bytes=60 * 2**20
+        ),
+    )(
+        tokens, positions.reshape(1, n_pos), value_proj, write_proj, read_proj, step_proj.T, step_bias.reshape(1, HEADS),
+        decay_rate.reshape(1, HEADS), reset_depth.reshape(1, ROWS), out_proj, router.reshape(1, D),
+        pad_vector.reshape(8, D // 8), up_weight, down_weight, cotangent,
+    )
+    half = ROWS // 2
     return pl.pallas_call(
-        functools.partial(kernel, zn, yn),
+        finish,
+        grid=(2,),
         out_shape=(
             jax.ShapeDtypeStruct((ROWS, D), BF16),
             jax.ShapeDtypeStruct((ru, D), F32),
             jax.ShapeDtypeStruct((rd, D), F32),
         ),
-        in_specs=[pl.BlockSpec(memory_space=pl.ANY)] * 15,
-        out_specs=(pl.BlockSpec(memory_space=pltpu.VMEM),) * 3,
-        scratch_shapes=scratch,
-        compiler_params=pltpu.CompilerParams(
-            collective_id=0, has_side_effects=True, vmem_limit_bytes=60 * 2**20
+        in_specs=[
+            pl.BlockSpec((half, D), lambda i: (i, 0)),
+            pl.BlockSpec((half, 2 * SLOTS), lambda i: (i, 0)),
+            pl.BlockSpec((SLOTS, D), lambda i: (0, 0)),
+            pl.BlockSpec((ru // 2, D), lambda i: (i, 0)),
+            pl.BlockSpec((rd // 2, D), lambda i: (i, 0)),
+        ],
+        out_specs=(
+            pl.BlockSpec((half, D), lambda i: (i, 0)),
+            pl.BlockSpec((ru // 2, D), lambda i: (i, 0)),
+            pl.BlockSpec((rd // 2, D), lambda i: (i, 0)),
         ),
-    )(
-        tokens, positions.reshape(1, n_pos), value_proj, write_proj, read_proj, step_proj, step_bias.reshape(1, HEADS),
-        decay_rate.reshape(1, HEADS), reset_depth.reshape(1, ROWS), out_proj, router.reshape(1, D),
-        pad_vector.reshape(1, D), up_weight, down_weight, cotangent,
-    )
+        compiler_params=pltpu.CompilerParams(vmem_limit_bytes=60 * 2**20),
+    )(encoded, mct, io, up_sum, down_sum)
 
 
 def solution(mesh):

time: 75.3 us -> 71.5 us (0.950)
  local copies, waits for them, and re-layouts: 6.47 us -> 0 us
  Pallas kernels: 68 us -> 70.7 us
    unnamed x8 -> x0, local copies, waits for them, and re-layouts: 5.19 us -> none
    pallas_call x0 -> x1, Pallas kernels: none -> 2.89 us  [on_device(): pl.pallas_call(finish, grid=(2,), out_shape=(jax.ShapeDtypeStruct((ROWS,...]
    reshape x1 -> x0, local copies, waits for them, and re-layouts: 1.28 us -> none  [on_device(): pad_vector.reshape(1, D)]
where the time goes in v2:
time: 71.5 us; the launch traced here: 71.4 us
  Pallas kernels  70.7 us (99%)
    pallas_call x1, Pallas kernels, on_device(): pl.pallas_call(functools.partial(kernel, zn, yn), out_shape=(jax.ShapeDty...  67.9 us
    pallas_call x1, Pallas kernels, on_device(): pl.pallas_call(finish, grid=(2,), out_shape=(jax.ShapeDtypeStruct((ROWS,...  2.89 us

profile of v2, /device:TPU:32, one launch (start us, length us, event | category | flops | bytes accessed | tf_op | source)
XLA Modules:
  0.0 71.4 jit_solution(16411969724970356791)
XLA Ops:
  0.6 67.9 %shard_map.166 = (bf16[512,1024]{1,0:T(8,128)(2,1)}, bf16[512,256]{1,0:T(8,128)(2,1)}, bf16[128,1024]{1,0:T(8,128)(2,1)}, f32[32,1024]{1,0:T(8,128)}, f32[16,1024]{1,0:T(8,128)}) custom-call(bf16[512,1024]{1,0:T(8,128)(2,1)} %tokens.1, s32[1,4096]{1,0:T(1,128)} %bitcast.8, bf16[1024,1024]{1,0:T(8,128)(2,1)} %value_proj.1, bf16[1024,128]{1,0:T(8,128)(2,1)} %write_proj.1, ...), custom_call_target="tpu_custom_call" | custom-call | tf_op jit(solution)/shard_map/pallas_call | solution.py:575
  68.5 2.9 %shard_map.167 = (bf16[512,1024]{1,0:T(8,128)(2,1)}, f32[32,1024]{1,0:T(8,128)}, f32[16,1024]{1,0:T(8,128)}) custom-call(bf16[512,1024]{1,0:T(8,128)(2,1)} %get-tuple-element.8.encoded, bf16[512,256]{1,0:T(8,128)(2,1)} %get-tuple-element.9.mct, bf16[128,1024]{1,0:T(8,128)(2,1)} %get-tuple-element.10.io, f32[32,1024]{1,0:T(8,128)} %get-tuple-element.11.up_sum, ...), custom_call_target="tpu_custom_call" | custom-call | tf_op jit(solution)/shard_map/pallas_call | solution.py:596

commit v3 on v2

--- a/solution.py
+++ b/solution.py
@@ -21,8 +21,12 @@
 SLOTS = 128
 XN, CN = 4, 2
 PLANE = XN * CN
-NQ = 4
+NQ = 8
+NZ = 2
+NX = NQ - NZ
 W = D // NQ
+ORDER = (0, 1, 2, 3, 0, 1, 4, 2, 0, 3, 1, 5, 4, 0, 2, 1, 3, 6, 0, 5, 2, 4, 7, 1, 6, 0, 3, 5, 2, 4, 7, 1, 3, 6, 0, 5, 4, 7, 1, 6, 5, 7, 6, 7)
+SHARE_AT, STORE_AT = 3, 20
 PIECE = 272
 EPS = 1e-05
 G0, G1 = 0.7978845608028654, 0.044715
@@ -61,7 +65,8 @@
     encoded, groups, select, mct, padup, pad_col, padsq,
     xn, gg, scale, slope, fac, turned, lt, lto, vx, vr,
     partial, ars, ar1, io,
-    own, prod, ra1, rb1, ra_left, ra_right, rb_left, rb_right, total, zs, zd, zu, zv,
+    own, prod, xa, xb, za_up, za_down, za_up_in, za_down_in, zb, zb_in,
+    prod_z, ring_up, ring_down, ring_up_in, ring_down_in, prod_x, xa_z, xb_z,
     load, store, ss, rs,
 ):
     sn = zn * PLANE
@@ -113,7 +118,7 @@
         )
 
     step1, step2, step3, from3, swaps, share1, share2, from2 = [], [None], [], [], [], [], [], []
-    ahead, later, along = [], [], []
+    copies = []
 
     for copy in loads[:7]:
         copy.wait()
@@ -329,23 +334,23 @@
     inner = rows_f * r
     xn[...] = inner.astype(BF16)
 
-    def turn(field, first_row, each, blocks):
+    def turn(field, part, each, blocks):
         turned[...] = field.T.astype(BF16)
         for k in range(XN):
             at = lax.rem(x + k, XN)
             for b in range(blocks):
-                rows = slice(first_row + b * each, first_row + (b + 1) * each)
+                rows = slice(b * each, (b + 1) * each)
                 begin = (b * PLANE + at * CN + core) * each
-                lt[k, rows, 0:SLOTS] = turned[pl.ds(pl.multiple_of(begin, 16), each), :]
+                lt[part, k, rows, 0:SLOTS] = turned[pl.ds(pl.multiple_of(begin, 16), each), :]
                 begin = (b * PLANE + at * CN + 1 - core) * each
-                lto[k, rows, :] = turned[pl.ds(pl.multiple_of(begin, 16), each), :]
+                lto[part, k, rows, :] = turned[pl.ds(pl.multiple_of(begin, 16), each), :]
 
     turn(inner, 0, ru, zh)
-    turn(grads, 128, rd, zn)
+    turn(grads, 1, rd, zn)
     mate = plane_at(x * CN + 1 - core)
     base = ids(4)
     swaps += [
-        rdma(lto, lt.at[:, :, SLOTS : 2 * SLOTS], base, mate, y),
+        rdma(lto, lt.at[:, :, :, SLOTS : 2 * SLOTS], base, mate, y),
         rdma(fac.at[1, 0:SLOTS, :], fac.at[1, SLOTS : 2 * SLOTS, :], base + 1, mate, y),
         rdma(fac.at[0, 0:SLOTS, :], fac.at[0, SLOTS : 2 * SLOTS, :], base + 2, mate, y),
         rdma(vx, vr, base + 3, mate, y),
@@ -396,68 +401,198 @@
         copy.wait_recv()
     right_x = plane_at(lax.rem(x + 1, XN) * CN + core)
     left_x = plane_at(lax.rem(x + XN - 1, XN) * CN + core)
-    upper, lower = slice(0, 128), slice(128, PIECE)
-    def multiply(q):
+
+    def on_z(o):
+        return lax.rem(z + o + zn, zn)
+
+    def device_z(o):
+        return on_z(o) * PLANE + me
+
+    def sent(*args):
+        copy = rdma(*args)
+        copy.start()
+        copies.append(copy)
+        return copy
+
+    def f32(block):
+        return block.astype(F32)
+
+    class AlongX:
+        def __init__(self, src, upper, lower, a_in, b_in):
+            self.src, self.upper, self.lower, self.a_in, self.b_in = src, upper, lower, a_in, b_in
+            self.base = ids(6)
+
+        def ahead(self):
+            src, up_rows, low_rows, i = self.src, self.upper, self.lower, self.base
+            self.far_a = sent(src.at[2, up_rows, :], self.a_in.at[0], i, right_x, y)
+            self.far_b = sent(src.at[2, low_rows, :], self.b_in.at[0], i + 1, left_x, y)
+            self.rest = [
+                sent(src.at[1, low_rows, :], self.b_in.at[1], i + 2, right_x, y),
+                sent(src.at[3, up_rows, :], self.a_in.at[1], i + 3, left_x, y),
+            ]
+
+        def later(self):
+            src, up_rows, low_rows, i = self.src, self.upper, self.lower, self.base
+            self.far_a.wait_recv()
+            src[1, up_rows, :] = (f32(src[1, up_rows, :]) + f32(self.a_in[0])).astype(BF16)
+            self.rest.append(sent(src.at[1, up_rows, :], self.a_in.at[2], i + 4, right_x, y))
+            self.far_b.wait_recv()
+            src[3, low_rows, :] = (f32(src[3, low_rows, :]) + f32(self.b_in[0])).astype(BF16)
+            self.rest.append(sent(src.at[3, low_rows, :], self.b_in.at[2], i + 5, left_x, y))
+
+        def arrived(self):
+            for copy in self.rest:
+                copy.wait_recv()
+            return f32(self.a_in[1]) + f32(self.a_in[2]), f32(self.b_in[1]) + f32(self.b_in[2])
+
+    def up_rows(t):
+        return pl.ds(pl.multiple_of(jnp.where(t < zh, ru * t, 256), 16), ru)
+
+    def down_rows(t):
+        return pl.ds(pl.multiple_of(128 + rd * t, 16), rd)
+
+    pad_part = pad_col[pl.ds(pl.multiple_of(ru * jnp.maximum(seq - sn // 2, 0), 16), ru), 0:1]
+
+    def write(q, up_sum, down_sum):
         cols = slice(q * W, (q + 1) * W)
-        pad_rows = in_rows([vx[0:1, cols] + vr[0:1, cols]], (16, W))
-        own[q, 256:PIECE, :] = pad_rows
-        for k in range(1, XN):
-            prod[k, q, 256:PIECE, :] = pad_rows.astype(BF16)
+        up_out[:, cols] = jnp.where(z < zh, up_sum, pad_part * up_sum[0:1])
+        down_out[:, cols] = down_sum
+
+    def terms(q):
+        cols = slice(q * W, (q + 1) * W)
         for part in range(2):
-            rows = slice(128 * part, 128 * part + 128)
-            for k in (2, 1, 3, 0):
-                term = nn(lt[k, rows, :], fac[part, :, cols])
-                if k:
-                    prod[k, q, rows, :] = term.astype(BF16)
+            yield nn(lt[part].reshape(XN * 128, 2 * SLOTS), fac[part, :, cols])
+        yield in_rows([vx[0:1, cols] + vr[0:1, cols]], (32, W))
+
+    def x_first(q):
+        n = q - NZ
+        along_x = AlongX(prod.at[n], slice(0, 128), slice(128, PIECE), xa.at[n], xb.at[n])
+        base = ids(6)
+
+        def piece(o):
+            t = on_z(o)
+            return own[n, up_rows(t), :], own[n, down_rows(t), :]
+
+        def first():
+            for part, term in enumerate(terms(q)):
+                if part < 2:
+                    rows = slice(128 * part, 128 * part + 128)
+                    own[n, rows, :] = term[0:128]
+                    for k in range(1, XN):
+                        prod[n, k, rows, :] = term[128 * k : 128 * k + 128].astype(BF16)
                 else:
-                    own[q, rows, :] = term
-
-    def send_ahead(q):
-        base = ids(4)
-        ahead.append([
-            rdma(prod.at[2, q, upper, :], ra1.at[q], base, right_x, y),
-            rdma(prod.at[2, q, lower, :], rb1.at[q], base + 1, left_x, y),
-            rdma(prod.at[1, q, lower, :], rb_left.at[q], base + 2, right_x, y),
-            rdma(prod.at[3, q, upper, :], ra_right.at[q], base + 3, left_x, y),
-        ])
-        for copy in ahead[q]:
-            copy.start()
-
-    def send_later(q):
-        base = ids(2)
-        later.append([
-            rdma(prod.at[1, q, upper, :], ra_left.at[q], base, right_x, y),
-            rdma(prod.at[3, q, lower, :], rb_right.at[q], base + 1, left_x, y),
-        ])
-        ahead[q][0].wait_recv()
-        prod[1, q, upper, :] = (prod[1, q, upper, :].astype(F32) + ra1[q].astype(F32)).astype(BF16)
-        later[q][0].start()
-        ahead[q][1].wait_recv()
-        prod[3, q, lower, :] = (prod[3, q, lower, :].astype(F32) + rb1[q].astype(F32)).astype(BF16)
-        later[q][1].start()
-
-    def send_along(q):
-        for copy in ahead[q][2:] + later[q]:
-            copy.wait_recv()
-        a = own[q, upper, :] + ra_left[q].astype(F32) + ra_right[q].astype(F32)
-        b = own[q, lower, :] + rb_left[q].astype(F32) + rb_right[q].astype(F32)
-        total[q, upper, :] = a
-        total[q, lower, :] = b
-        zs[q, upper, :] = a.astype(BF16)
-        zs[q, lower, :] = b.astype(BF16)
-        base = ids(2 * zn)
-        for o in range(1, zn):
-            to = lax.rem(z + o, zn)
-            dev = to * PLANE + me
-            up_rows = pl.ds(pl.multiple_of(ru * jnp.minimum(to, zh - 1), 16), ru)
-            down_rows = pl.ds(pl.multiple_of(128 + rd * to, 16), rd)
-            c_down = rdma(zs.at[q, down_rows, :], zd.at[q, o - 1], base + o, dev, y)
-            c_up = rdma(zs.at[q, up_rows, :], zu.at[q, o - 1], base + zn + o, dev, y)
-            c_pad = rdma(zs.at[q, 256:PIECE, :], zv.at[q, o - 1], base + zn + o, dev, y)
-            pl.when(to < zh)(c_up.start)
-            pl.when(to >= zh)(c_pad.start)
-            c_down.start()
-            along.append((q, to, c_down, c_up, c_pad))
+                    own[n, 256:288, :] = term
+                    for k in range(1, XN):
+                        prod[n, k, 256:PIECE, :] = term[0:16].astype(BF16)
+            along_x.ahead()
+
+        def two_away():
+            a, b = along_x.arrived()
+            own[n, 0:128, :] += a
+            own[n, 128:PIECE, :] += b
+            za_up[n, 0:32, :] = piece(4)[0].astype(BF16)
+            near = piece(3)
+            za_up[n, 32:64, :] = near[0].astype(BF16)
+            za_up[n, 64:80, :] = near[1].astype(BF16)
+            far.append(sent(za_up.at[n], za_up_in.at[n], base, device_z(2), y))
+            za_down[n, 0:16, :] = piece(-4)[1].astype(BF16)
+            near = piece(-3)
+            za_down[n, 16:32, :] = near[1].astype(BF16)
+            za_down[n, 32:64, :] = near[0].astype(BF16)
+            far.append(sent(za_down.at[n], za_down_in.at[n], base + 1, device_z(-2), y))
+
+        far, last = [], []
+
+        def nearer():
+            for copy in far:
+                copy.wait_recv()
+            from_up, from_down = f32(za_up_in[n]), f32(za_down_in[n])
+            for i, o in enumerate((2, -2, 1, -1)):
+                up_sum, down_sum = piece(o)
+                if o == 2:
+                    up_sum = up_sum + from_up[0:32]
+                elif o == -2:
+                    down_sum = down_sum + from_down[0:16]
+                elif o == 1:
+                    up_sum, down_sum = up_sum + from_up[32:64], down_sum + from_up[64:80]
+                else:
+                    up_sum, down_sum = up_sum + from_down[32:64], down_sum + from_down[16:32]
+                zb[n, i, 0:32, :] = up_sum.astype(BF16)
+                zb[n, i, 32:48, :] = down_sum.astype(BF16)
+                last.append(sent(zb.at[n, i], zb_in.at[n, i], base + 2 + i, device_z(o), y))
+
+        def final():
+            for copy in last:
+                copy.wait_recv()
+            up_sum, down_sum = piece(0)
+            for i in range(4):
+                up_sum = up_sum + f32(zb_in[n, i, 0:32, :])
+                down_sum = down_sum + f32(zb_in[n, i, 32:48, :])
+            write(q, up_sum, down_sum)
+
+        return [first, along_x.later, two_away, nearer, final]
+
+    def z_first(n):
+        along_x = AlongX(prod_x.at[n], slice(0, 32), slice(32, 48), xa_z.at[n], xb_z.at[n])
+        base = ids(8)
+        up_copy, down_copy = [], []
+
+        def piece(o):
+            t = on_z(o)
+            return prod_z[n, :, up_rows(t), :], prod_z[n, :, down_rows(t), :]
+
+        def hop(i):
+            if i == 0:
+                for part, term in enumerate(terms(n)):
+                    for k in range(XN):
+                        if part < 2:
+                            prod_z[n, k, 128 * part : 128 * part + 128, :] = term[128 * k : 128 * k + 128]
+                        else:
+                            prod_z[n, k, 256:288, :] = term
+                ring_up[n, 0, :, 0:32, :] = piece(4)[0].astype(BF16)
+                ring_down[n, 0, :, 32:48, :] = piece(-4)[1].astype(BF16)
+                rows_up, rows_down = slice(0, 32), slice(32, 48)
+            else:
+                up_copy[i - 1].wait_recv()
+                up_sum, down_sum = piece(4 - i)
+                up_sum = up_sum + f32(ring_up_in[n, i - 1, :, 0:32, :])
+                if i > 1:
+                    down_sum = down_sum + f32(ring_up_in[n, i - 1, :, 32:48, :])
+                ring_up[n, i, :, 0:32, :] = up_sum.astype(BF16)
+                ring_up[n, i, :, 32:48, :] = down_sum.astype(BF16)
+                down_copy[i - 1].wait_recv()
+                up_sum, down_sum = piece(i - 4)
+                down_sum = down_sum + f32(ring_down_in[n, i - 1, :, 32:48, :])
+                if i > 1:
+                    up_sum = up_sum + f32(ring_down_in[n, i - 1, :, 0:32, :])
+                ring_down[n, i, :, 0:32, :] = up_sum.astype(BF16)
+                ring_down[n, i, :, 32:48, :] = down_sum.astype(BF16)
+                rows_up = rows_down = slice(0, 48)
+            up_copy.append(
+                sent(ring_up.at[n, i, :, rows_up, :], ring_up_in.at[n, i, :, rows_up, :], base + i, device_z(1), y)
+            )
+            down_copy.append(
+                sent(ring_down.at[n, i, :, rows_down, :], ring_down_in.at[n, i, :, rows_down, :], base + 4 + i, device_z(-1), y)
+            )
+
+        mine_z = []
+
+        def collect():
+            up_copy[3].wait_recv()
+            down_copy[3].wait_recv()
+            up_sum, down_sum = piece(0)
+            up_sum = up_sum + f32(ring_up_in[n, 3, :, 0:32, :]) + f32(ring_down_in[n, 3, :, 0:32, :])
+            down_sum = down_sum + f32(ring_up_in[n, 3, :, 32:48, :]) + f32(ring_down_in[n, 3, :, 32:48, :])
+            prod_x[n, :, 0:32, :] = up_sum.astype(BF16)
+            prod_x[n, :, 32:48, :] = down_sum.astype(BF16)
+            mine_z.extend([up_sum[0], down_sum[0]])
+            along_x.ahead()
+
+        def final():
+            a, b = along_x.arrived()
+            write(n, mine_z[0] + a, mine_z[1] + b)
+
+        return [functools.partial(hop, i) for i in range(4)] + [collect, along_x.later, final]
 
     def reduce_share():
         for copy in share1:
@@ -475,49 +610,13 @@
         stores.append(pltpu.make_async_copy(io, io_out, store.at[2]))
         stores[2].start()
 
-    multiply(0)
-    send_ahead(0)
-    multiply(1)
-    send_ahead(1)
-    reduce_share()
-    send_later(0)
-    for q in range(2, NQ):
-        multiply(q)
-        send_ahead(q)
-        send_later(q - 1)
-        if q == 2:
+    steps = [iter(z_first(q) if q < NZ else x_first(q)) for q in range(NQ)]
+    for i, q in enumerate(ORDER):
+        if i == SHARE_AT:
+            reduce_share()
+        if i == STORE_AT:
             share()
-        send_along(q - 2)
-    send_later(NQ - 1)
-    send_along(NQ - 2)
-    send_along(NQ - 1)
-
-    pad_part = pad_col[pl.ds(pl.multiple_of(ru * jnp.maximum(seq - sn // 2, 0), 16), ru), 0:1]
-    for q in range(NQ):
-        cols = slice(q * W, (q + 1) * W)
-        for at, to, c_down, c_up, c_pad in along:
-            if at == q:
-                c_down.wait_recv()
-                pl.when(z < zh)(c_up.wait_recv)
-                pl.when(z >= zh)(c_pad.wait_recv)
-        down_sum = total[q, pl.ds(pl.multiple_of(128 + rd * z, 16), rd), :]
-        for o in range(zn - 1):
-            down_sum = down_sum + zd[q, o].astype(F32)
-        down_out[:, cols] = down_sum
-
-        @pl.when(z < zh)
-        def _():
-            up_sum = total[q, pl.ds(pl.multiple_of(ru * jnp.minimum(z, zh - 1), 16), ru), :]
-            for o in range(zn - 1):
-                up_sum = up_sum + zu[q, o].astype(F32)
-            up_out[:, cols] = up_sum
-
-        @pl.when(z >= zh)
-        def _():
-            pad_sum = total[q, 256:257, :]
-            for o in range(zn - 1):
-                pad_sum = pad_sum + zv[q, o, 0:1, :].astype(F32)
-            up_out[:, cols] = pad_part * pad_sum
+        next(steps[q])()
 
     for copy in stores:
         copy.wait()
@@ -525,13 +624,8 @@
         copy.wait_send()
     for o in range(1, len(step2)):
         pl.when(z + o < zn)(step2[o].wait_send)
-    for copies in ahead + later:
-        for copy in copies:
-            copy.wait_send()
-    for q, to, c_down, c_up, c_pad in along:
-        c_down.wait_send()
-        pl.when(to < zh)(c_up.wait_send)
-        pl.when(to >= zh)(c_pad.wait_send)
+    for copy in copies:
+        copy.wait_send()
 
 
 def finish(encoded, mct, io, up_sum, down_sum, mixed, up_out, down_out):
@@ -550,7 +644,7 @@
     ru, rd, qw = 2 * D // sn, D // sn, D // yn
     n_pos = positions.shape[0]
     vm = pltpu.VMEM
-    n_sem = PLANE + zn + PLANE * yn + 4 + 2 * yn + NQ * (6 + 2 * zn)
+    n_sem = PLANE + zn + PLANE * yn + 4 + 2 * yn + NX * 12 + NZ * 14
     scratch = [
         vm((ROWS, D), BF16), vm((1, n_pos), jnp.int32), vm((D, D), BF16), vm((D, 2 * NS), BF16), vm((HEADS, D), BF16),
         vm((1, HEADS), F32), vm((1, HEADS), F32), vm((1, ROWS), F32), vm((D, D), BF16), vm((1, D), F32),
@@ -563,13 +657,16 @@
         vm((ROWS, D), BF16), vm((SLOTS, D), F32), vm((SLOTS, ROWS), BF16), vm((ROWS, 2 * SLOTS), BF16),
         vm((16, D), F32), vm((D, 128), F32), vm((8, 128), F32),
         vm((SLOTS, D), BF16), vm((SLOTS, D), BF16), vm((SLOTS, 128), F32), vm((SLOTS, D), F32),
-        vm((2, 2 * SLOTS, D), BF16), vm((D, SLOTS), BF16), vm((XN, 256, 2 * SLOTS), BF16), vm((XN, 256, SLOTS), BF16),
+        vm((2, 2 * SLOTS, D), BF16), vm((D, SLOTS), BF16), vm((2, XN, 128, 2 * SLOTS), BF16),
+        vm((2, XN, 128, SLOTS), BF16),
         vm((8, D), F32), vm((8, D), F32),
         vm((SLOTS, D), F32), vm((SLOTS, D), BF16), vm((max(yn - 1, 1), SLOTS // yn, D), BF16), vm((SLOTS, D), BF16),
-        vm((NQ, PIECE, W), F32), vm((XN, NQ, PIECE, W), BF16), vm((NQ, 128, W), BF16), vm((NQ, 144, W), BF16),
-        vm((NQ, 128, W), BF16), vm((NQ, 128, W), BF16), vm((NQ, 144, W), BF16), vm((NQ, 144, W), BF16),
-        vm((NQ, PIECE, W), F32), vm((NQ, PIECE, W), BF16), vm((NQ, zn - 1, rd, W), BF16), vm((NQ, zn - 1, ru, W), BF16),
-        vm((NQ, zn - 1, 16, W), BF16),
+        vm((NX, 288, W), F32), vm((NX, XN, PIECE, W), BF16), vm((NX, 3, 128, W), BF16), vm((NX, 3, 144, W), BF16),
+        vm((NX, 80, W), BF16), vm((NX, 64, W), BF16), vm((NX, 80, W), BF16), vm((NX, 64, W), BF16),
+        vm((NX, 4, 48, W), BF16), vm((NX, 4, 48, W), BF16),
+        vm((NZ, XN, 288, W), F32), vm((NZ, 4, XN, 48, W), BF16), vm((NZ, 4, XN, 48, W), BF16),
+        vm((NZ, 4, XN, 48, W), BF16), vm((NZ, 4, XN, 48, W), BF16), vm((NZ, XN, 48, W), BF16),
+        vm((NZ, 3, 32, W), BF16), vm((NZ, 3, 16, W), BF16),
         pltpu.SemaphoreType.DMA((15,)), pltpu.SemaphoreType.DMA((3,)), pltpu.SemaphoreType.DMA((n_sem,)), pltpu.SemaphoreType.DMA((n_sem,)),
     ]
     encoded, mct, io, up_sum, down_sum = pl.pallas_call(

time: 71.5 us -> 75.7 us (1.059)
  Pallas kernels: 70.7 us -> 74.4 us
    pallas_call x1, Pallas kernels: 67.9 us -> 71.5 us  [on_device(): pl.pallas_call(functools.partial(kernel, zn, yn), out_shape=(jax.ShapeDty...]
where the time goes in v3:
time: 75.7 us; the launch traced here: 75 us
  Pallas kernels  74.4 us (98%)
    pallas_call x1, Pallas kernels, on_device(): pl.pallas_call(functools.partial(kernel, zn, yn), out_shape=(jax.ShapeDty...  71.5 us
    pallas_call x1, Pallas kernels, on_device(): pl.pallas_call(finish, grid=(2,), out_shape=(jax.ShapeDtypeStruct((ROWS,...  2.89 us

profile of v3, /device:TPU:32, one launch (start us, length us, event | category | flops | bytes accessed | tf_op | source)
XLA Modules:
  0.0 75.0 jit_solution(3099885335480080942)
XLA Ops:
  0.6 71.5 %shard_map.166 = (bf16[512,1024]{1,0:T(8,128)(2,1)}, bf16[512,256]{1,0:T(8,128)(2,1)}, bf16[128,1024]{1,0:T(8,128)(2,1)}, f32[32,1024]{1,0:T(8,128)}, f32[16,1024]{1,0:T(8,128)}) custom-call(bf16[512,1024]{1,0:T(8,128)(2,1)} %tokens.1, s32[1,4096]{1,0:T(1,128)} %bitcast.8, bf16[1024,1024]{1,0:T(8,128)(2,1)} %value_proj.1, bf16[1024,128]{1,0:T(8,128)(2,1)} %write_proj.1, ...), custom_call_target="tpu_custom_call" | custom-call | tf_op jit(solution)/shard_map/pallas_call | solution.py:672
  72.1 2.9 %shard_map.167 = (bf16[512,1024]{1,0:T(8,128)(2,1)}, f32[32,1024]{1,0:T(8,128)}, f32[16,1024]{1,0:T(8,128)}) custom-call(bf16[512,1024]{1,0:T(8,128)(2,1)} %get-tuple-element.8.encoded, bf16[512,256]{1,0:T(8,128)(2,1)} %get-tuple-element.9.mct, bf16[128,1024]{1,0:T(8,128)(2,1)} %get-tuple-element.10.io, f32[32,1024]{1,0:T(8,128)} %get-tuple-element.11.up_sum, ...), custom_call_target="tpu_custom_call" | custom-call | tf_op jit(solution)/shard_map/pallas_call | solution.py:693

commit v4 on v3

--- a/solution.py
+++ b/solution.py
@@ -21,11 +21,11 @@
 SLOTS = 128
 XN, CN = 4, 2
 PLANE = XN * CN
-NQ = 8
-NZ = 2
-NX = NQ - NZ
-W = D // NQ
-ORDER = (0, 1, 2, 3, 0, 1, 4, 2, 0, 3, 1, 5, 4, 0, 2, 1, 3, 6, 0, 5, 2, 4, 7, 1, 6, 0, 3, 5, 2, 4, 7, 1, 3, 6, 0, 5, 4, 7, 1, 6, 5, 7, 6, 7)
+WIDTHS_Z, WIDTHS_X = (128, 128), (256, 256, 128, 128)
+NZ, NQ = len(WIDTHS_Z), len(WIDTHS_Z + WIDTHS_X)
+ORDER = (
+    3, 0, 1, 2, 0, 1, 3, 0, 5, 1, 2, 3, 4, 1, 5, 0, 2, 3, 4, 1, 5, 0, 4, 2, 0, 3, 1, 5, 4, 1, 0, 2, 5, 4,
+)
 SHARE_AT, STORE_AT = 3, 20
 PIECE = 272
 EPS = 1e-05
@@ -65,8 +65,7 @@
     encoded, groups, select, mct, padup, pad_col, padsq,
     xn, gg, scale, slope, fac, turned, lt, lto, vx, vr,
     partial, ars, ar1, io,
-    own, prod, xa, xb, za_up, za_down, za_up_in, za_down_in, zb, zb_in,
-    prod_z, ring_up, ring_down, ring_up_in, ring_down_in, prod_x, xa_z, xb_z,
+    along_z, along_x,
     load, store, ss, rs,
 ):
     sn = zn * PLANE
@@ -90,20 +89,11 @@
         copy.start()
 
     barrier = pltpu.get_barrier_semaphore()
-    peers = 0
-    for oy in range(yn):
-        for o in range(PLANE):
-            if o or oy:
-                peers += 1
-                pl.semaphore_signal(
-                    barrier, inc=1, device_id_type=MESH,
-                    device_id=(plane_at(lax.rem(me + o, PLANE)), lax.rem(y + oy, yn)),
-                )
-    for o in range(1, zn):
-        peers += 1
-        pl.semaphore_signal(
-            barrier, inc=1, device_id_type=MESH, device_id=(lax.rem(z + o, zn) * PLANE + me, y)
-        )
+    partners = [(plane_at(lax.rem(me + o, PLANE)), y) for o in range(1, PLANE)]
+    partners += [(lax.rem(z + o, zn) * PLANE + me, y) for o in range(1, zn)]
+    partners += [(seq, lax.rem(y + o, yn)) for o in range(1, yn)]
+    for partner in partners:
+        pl.semaphore_signal(barrier, inc=1, device_id=partner, device_id_type=MESH)
 
     count = [0]
 
@@ -200,7 +190,7 @@
         p1s[j, 0:16, :] = state[16 * j : 16 * j + 16, mine].astype(BF16)
         p1s[j, 16:32, :] = decay_rows
     p1r[0] = p1s[me]
-    pl.semaphore_wait(barrier, peers)
+    pl.semaphore_wait(barrier, len(partners))
     base = ids(PLANE)
     for o in range(1, PLANE):
         j = lax.rem(me + o, PLANE)
@@ -259,17 +249,25 @@
     def landing(j, at_y):
         return incoming.at[pl.ds(pl.multiple_of(j * 16, 16), 16), pl.ds(pl.multiple_of(at_y * qw, qw), qw)]
 
-    base = ids(PLANE * yn)
-    for o in range(PLANE):
-        for oy in range(yn):
-            if o or oy:
-                i = base + o * yn + oy
-                j, at_y = lax.rem(me + o, PLANE), lax.rem(y + oy, yn)
-                step3.append(rdma(p3s.at[j], landing(me, y), i, plane_at(j), at_y))
-                step3[-1].start()
-                j, at_y = lax.rem(me - o + PLANE, PLANE), lax.rem(y - oy + yn, yn)
-                from3.append(rdma(p3s.at[j], landing(j, at_y), i, plane_at(j), at_y))
+    base = ids(PLANE + yn)
+    for o in range(1, PLANE):
+        j = lax.rem(me + o, PLANE)
+        step3.append(rdma(p3s.at[j], landing(me, y), base + o, plane_at(j), y))
+        step3[-1].start()
+        j = lax.rem(me - o + PLANE, PLANE)
+        from3.append(rdma(p3s.at[j], landing(j, y), base + o, plane_at(j), y))
     incoming[pl.ds(pl.multiple_of(me * 16, 16), 16), mine] = p3s[me]
+
+    for copy in from3:
+        copy.wait_recv()
+    from3.clear()
+    for o in range(1, yn):
+        at_y = lax.rem(y + o, yn)
+        step3.append(rdma(incoming.at[:, mine], incoming.at[:, mine], base + PLANE + o, seq, at_y))
+        step3[-1].start()
+        at_y = lax.rem(y - o + yn, yn)
+        theirs = incoming.at[:, pl.ds(pl.multiple_of(at_y * qw, qw), qw)]
+        from3.append(rdma(theirs, theirs, base + PLANE + o, seq, at_y))
 
     for copy in loads[8:]:
         copy.wait()
@@ -418,32 +416,35 @@
         return block.astype(F32)
 
     class AlongX:
-        def __init__(self, src, upper, lower, a_in, b_in):
-            self.src, self.upper, self.lower, self.a_in, self.b_in = src, upper, lower, a_in, b_in
-            self.base = ids(6)
+        def __init__(self, upper, lower, refs):
+            self.near_r, self.near_l, self.end_r, self.end_l = refs[:4]
+            self.near_r_in, self.near_l_in, self.end_r_in, self.end_l_in = refs[4:]
+            self.cut_r, self.cut_l = upper, lower
+            self.up = {1: self.end_r, 2: self.near_r.at[0:upper, :], 3: self.near_l.at[lower:, :]}
+            self.low = {1: self.near_r.at[upper:, :], 2: self.near_l.at[0:lower, :], 3: self.end_l}
+            self.base = ids(4)
 
         def ahead(self):
-            src, up_rows, low_rows, i = self.src, self.upper, self.lower, self.base
-            self.far_a = sent(src.at[2, up_rows, :], self.a_in.at[0], i, right_x, y)
-            self.far_b = sent(src.at[2, low_rows, :], self.b_in.at[0], i + 1, left_x, y)
-            self.rest = [
-                sent(src.at[1, low_rows, :], self.b_in.at[1], i + 2, right_x, y),
-                sent(src.at[3, up_rows, :], self.a_in.at[1], i + 3, left_x, y),
+            self.near = [
+                sent(self.near_r, self.near_r_in, self.base, right_x, y),
+                sent(self.near_l, self.near_l_in, self.base + 1, left_x, y),
             ]
 
         def later(self):
-            src, up_rows, low_rows, i = self.src, self.upper, self.lower, self.base
-            self.far_a.wait_recv()
-            src[1, up_rows, :] = (f32(src[1, up_rows, :]) + f32(self.a_in[0])).astype(BF16)
-            self.rest.append(sent(src.at[1, up_rows, :], self.a_in.at[2], i + 4, right_x, y))
-            self.far_b.wait_recv()
-            src[3, low_rows, :] = (f32(src[3, low_rows, :]) + f32(self.b_in[0])).astype(BF16)
-            self.rest.append(sent(src.at[3, low_rows, :], self.b_in.at[2], i + 5, left_x, y))
+            self.near[0].wait_recv()
+            self.end_r[...] = (f32(self.end_r[...]) + f32(self.near_r_in[0 : self.cut_r, :])).astype(BF16)
+            first = sent(self.end_r, self.end_r_in, self.base + 2, right_x, y)
+            self.near[1].wait_recv()
+            self.end_l[...] = (f32(self.end_l[...]) + f32(self.near_l_in[0 : self.cut_l, :])).astype(BF16)
+            self.end = [first, sent(self.end_l, self.end_l_in, self.base + 3, left_x, y)]
 
         def arrived(self):
-            for copy in self.rest:
+            for copy in self.end:
                 copy.wait_recv()
-            return f32(self.a_in[1]) + f32(self.a_in[2]), f32(self.b_in[1]) + f32(self.b_in[2])
+            return (
+                f32(self.near_l_in[self.cut_l :, :]) + f32(self.end_r_in[...]),
+                f32(self.near_r_in[self.cut_r :, :]) + f32(self.end_l_in[...]),
+            )
 
     def up_rows(t):
         return pl.ds(pl.multiple_of(jnp.where(t < zh, ru * t, 256), 16), ru)
@@ -453,60 +454,65 @@
 
     pad_part = pad_col[pl.ds(pl.multiple_of(ru * jnp.maximum(seq - sn // 2, 0), 16), ru), 0:1]
 
+    widths = WIDTHS_Z + WIDTHS_X
+
+    def columns(q):
+        return slice(sum(widths[:q]), sum(widths[: q + 1]))
+
     def write(q, up_sum, down_sum):
-        cols = slice(q * W, (q + 1) * W)
+        cols = columns(q)
         up_out[:, cols] = jnp.where(z < zh, up_sum, pad_part * up_sum[0:1])
         down_out[:, cols] = down_sum
 
     def terms(q):
-        cols = slice(q * W, (q + 1) * W)
+        cols = columns(q)
         for part in range(2):
             yield nn(lt[part].reshape(XN * 128, 2 * SLOTS), fac[part, :, cols])
-        yield in_rows([vx[0:1, cols] + vr[0:1, cols]], (32, W))
+        yield in_rows([vx[0:1, cols] + vr[0:1, cols]], (32, widths[q]))
 
     def x_first(q):
-        n = q - NZ
-        along_x = AlongX(prod.at[n], slice(0, 128), slice(128, PIECE), xa.at[n], xb.at[n])
+        own, za_up, za_down, za_up_in, za_down_in, zb, zb_in, *rest = along_x[q - NZ]
+        by_x = AlongX(128, 144, rest)
         base = ids(6)
 
         def piece(o):
             t = on_z(o)
-            return own[n, up_rows(t), :], own[n, down_rows(t), :]
+            return own[up_rows(t), :], own[down_rows(t), :]
 
         def first():
             for part, term in enumerate(terms(q)):
                 if part < 2:
                     rows = slice(128 * part, 128 * part + 128)
-                    own[n, rows, :] = term[0:128]
+                    own[rows, :] = term[0:128]
                     for k in range(1, XN):
-                        prod[n, k, rows, :] = term[128 * k : 128 * k + 128].astype(BF16)
+                        (by_x.low if part else by_x.up)[k][0:128, :] = term[128 * k : 128 * k + 128].astype(BF16)
                 else:
-                    own[n, 256:288, :] = term
+                    own[256:288, :] = term
                     for k in range(1, XN):
-                        prod[n, k, 256:PIECE, :] = term[0:16].astype(BF16)
-            along_x.ahead()
+                        by_x.low[k][128:144, :] = term[0:16].astype(BF16)
+            by_x.ahead()
 
         def two_away():
-            a, b = along_x.arrived()
-            own[n, 0:128, :] += a
-            own[n, 128:PIECE, :] += b
-            za_up[n, 0:32, :] = piece(4)[0].astype(BF16)
+            a, b = by_x.arrived()
+            own[0:128, :] += a
+            own[128:PIECE, :] += b
+            za_up[0:32, :] = piece(4)[0].astype(BF16)
             near = piece(3)
-            za_up[n, 32:64, :] = near[0].astype(BF16)
-            za_up[n, 64:80, :] = near[1].astype(BF16)
-            far.append(sent(za_up.at[n], za_up_in.at[n], base, device_z(2), y))
-            za_down[n, 0:16, :] = piece(-4)[1].astype(BF16)
+            za_up[32:64, :] = near[0].astype(BF16)
+            za_up[64:80, :] = near[1].astype(BF16)
+            far.append(sent(za_up, za_up_in, base, device_z(2), y))
+            za_down[0:16, :] = piece(-4)[1].astype(BF16)
             near = piece(-3)
-            za_down[n, 16:32, :] = near[1].astype(BF16)
-            za_down[n, 32:64, :] = near[0].astype(BF16)
-            far.append(sent(za_down.at[n], za_down_in.at[n], base + 1, device_z(-2), y))
+            za_down[16:32, :] = near[1].astype(BF16)
+            za_down[32:64, :] = near[0].astype(BF16)
+            far.append(sent(za_down, za_down_in, base + 1, device_z(-2), y))
 
         far, last = [], []
 
         def nearer():
             for copy in far:
                 copy.wait_recv()
-            from_up, from_down = f32(za_up_in[n]), f32(za_down_in[n])
+            from_up, from_down = f32(za_up_in[...]), f32(za_down_in[...])
             for i, o in enumerate((2, -2, 1, -1)):
                 up_sum, down_sum = piece(o)
                 if o == 2:
@@ -517,62 +523,63 @@
                     up_sum, down_sum = up_sum + from_up[32:64], down_sum + from_up[64:80]
                 else:
                     up_sum, down_sum = up_sum + from_down[32:64], down_sum + from_down[16:32]
-                zb[n, i, 0:32, :] = up_sum.astype(BF16)
-                zb[n, i, 32:48, :] = down_sum.astype(BF16)
-                last.append(sent(zb.at[n, i], zb_in.at[n, i], base + 2 + i, device_z(o), y))
+                zb[i, 0:32, :] = up_sum.astype(BF16)
+                zb[i, 32:48, :] = down_sum.astype(BF16)
+                last.append(sent(zb.at[i], zb_in.at[i], base + 2 + i, device_z(o), y))
 
         def final():
             for copy in last:
                 copy.wait_recv()
             up_sum, down_sum = piece(0)
             for i in range(4):
-                up_sum = up_sum + f32(zb_in[n, i, 0:32, :])
-                down_sum = down_sum + f32(zb_in[n, i, 32:48, :])
+                up_sum = up_sum + f32(zb_in[i, 0:32, :])
+                down_sum = down_sum + f32(zb_in[i, 32:48, :])
             write(q, up_sum, down_sum)
 
-        return [first, along_x.later, two_away, nearer, final]
+        return [first, by_x.later, two_away, nearer, final]
 
     def z_first(n):
-        along_x = AlongX(prod_x.at[n], slice(0, 32), slice(32, 48), xa_z.at[n], xb_z.at[n])
+        prod_z, ring_up, ring_down, ring_up_in, ring_down_in, *rest = along_z[n]
+        by_x = AlongX(32, 16, rest)
         base = ids(8)
         up_copy, down_copy = [], []
 
         def piece(o):
             t = on_z(o)
-            return prod_z[n, :, up_rows(t), :], prod_z[n, :, down_rows(t), :]
+            return prod_z[:, up_rows(t), :], prod_z[:, down_rows(t), :]
 
         def hop(i):
             if i == 0:
                 for part, term in enumerate(terms(n)):
                     for k in range(XN):
                         if part < 2:
-                            prod_z[n, k, 128 * part : 128 * part + 128, :] = term[128 * k : 128 * k + 128]
+                            prod_z[k, 128 * part : 128 * part + 128, :] = term[128 * k : 128 * k + 128]
                         else:
-                            prod_z[n, k, 256:288, :] = term
-                ring_up[n, 0, :, 0:32, :] = piece(4)[0].astype(BF16)
-                ring_down[n, 0, :, 32:48, :] = piece(-4)[1].astype(BF16)
+                            prod_z[k, 256:288, :] = term
+                ring_up[0, :, 0:32, :] = piece(4)[0].astype(BF16)
+                ring_down[0, :, 32:48, :] = piece(-4)[1].astype(BF16)
                 rows_up, rows_down = slice(0, 32), slice(32, 48)
             else:
                 up_copy[i - 1].wait_recv()
                 up_sum, down_sum = piece(4 - i)
-                up_sum = up_sum + f32(ring_up_in[n, i - 1, :, 0:32, :])
+                up_sum = up_sum + f32(ring_up_in[i - 1, :, 0:32, :])
                 if i > 1:
-                    down_sum = down_sum + f32(ring_up_in[n, i - 1, :, 32:48, :])
-                ring_up[n, i, :, 0:32, :] = up_sum.astype(BF16)
-                ring_up[n, i, :, 32:48, :] = down_sum.astype(BF16)
+                    down_sum = down_sum + f32(ring_up_in[i - 1, :, 32:48, :])
+                ring_up[i, :, 0:32, :] = up_sum.astype(BF16)
+                ring_up[i, :, 32:48, :] = down_sum.astype(BF16)
                 down_copy[i - 1].wait_recv()
                 up_sum, down_sum = piece(i - 4)
-                down_sum = down_sum + f32(ring_down_in[n, i - 1, :, 32:48, :])
+                down_sum = down_sum + f32(ring_down_in[i - 1, :, 32:48, :])
                 if i > 1:
-                    up_sum = up_sum + f32(ring_down_in[n, i - 1, :, 0:32, :])
-                ring_down[n, i, :, 0:32, :] = up_sum.astype(BF16)
-                ring_down[n, i, :, 32:48, :] = down_sum.astype(BF16)
+                    up_sum = up_sum + f32(ring_down_in[i - 1, :, 0:32, :])
+                ring_down[i, :, 0:32, :] = up_sum.astype(BF16)
+                ring_down[i, :, 32:48, :] = down_sum.astype(BF16)
                 rows_up = rows_down = slice(0, 48)
             up_copy.append(
-                sent(ring_up.at[n, i, :, rows_up, :], ring_up_in.at[n, i, :, rows_up, :], base + i, device_z(1), y)
+                sent(ring_up.at[i, :, rows_up, :], ring_up_in.at[i, :, rows_up, :], base + i, device_z(1), y)
             )
             down_copy.append(
-                sent(ring_down.at[n, i, :, rows_down, :], ring_down_in.at[n, i, :, rows_down, :], base + 4 + i, device_z(-1), y)
+                sent(ring_down.at[i, :, rows_down, :], ring_down_in.at[i, :, rows_down, :], base + 4 + i, device_z(-1), y)
             )
 
         mine_z = []
@@ -581,18 +588,19 @@
             up_copy[3].wait_recv()
             down_copy[3].wait_recv()
             up_sum, down_sum = piece(0)
-            up_sum = up_sum + f32(ring_up_in[n, 3, :, 0:32, :]) + f32(ring_down_in[n, 3, :, 0:32, :])
-            down_sum = down_sum + f32(ring_up_in[n, 3, :, 32:48, :]) + f32(ring_down_in[n, 3, :, 32:48, :])
-            prod_x[n, :, 0:32, :] = up_sum.astype(BF16)
-            prod_x[n, :, 32:48, :] = down_sum.astype(BF16)
+            up_sum = up_sum + f32(ring_up_in[3, :, 0:32, :]) + f32(ring_down_in[3, :, 0:32, :])
+            down_sum = down_sum + f32(ring_up_in[3, :, 32:48, :]) + f32(ring_down_in[3, :, 32:48, :])
+            for k in range(1, XN):
+                by_x.up[k][...] = up_sum[k].astype(BF16)
+                by_x.low[k][...] = down_sum[k].astype(BF16)
             mine_z.extend([up_sum[0], down_sum[0]])
-            along_x.ahead()
+            by_x.ahead()
 
         def final():
-            a, b = along_x.arrived()
+            a, b = by_x.arrived()
             write(n, mine_z[0] + a, mine_z[1] + b)
 
-        return [functools.partial(hop, i) for i in range(4)] + [collect, along_x.later, final]
+        return [functools.partial(hop, i) for i in range(4)] + [collect, by_x.later, final]
 
     def reduce_share():
         for copy in share1:
@@ -644,7 +652,7 @@
     ru, rd, qw = 2 * D // sn, D // sn, D // yn
     n_pos = positions.shape[0]
     vm = pltpu.VMEM
-    n_sem = PLANE + zn + PLANE * yn + 4 + 2 * yn + NX * 12 + NZ * 14
+    n_sem = 2 * PLANE + zn + 4 + 3 * yn + NQ * 14
     scratch = [
         vm((ROWS, D), BF16), vm((1, n_pos), jnp.int32), vm((D, D), BF16), vm((D, 2 * NS), BF16), vm((HEADS, D), BF16),
         vm((1, HEADS), F32), vm((1, HEADS), F32), vm((1, ROWS), F32), vm((D, D), BF16), vm((1, D), F32),
@@ -661,12 +669,14 @@
         vm((2, XN, 128, SLOTS), BF16),
         vm((8, D), F32), vm((8, D), F32),
         vm((SLOTS, D), F32), vm((SLOTS, D), BF16), vm((max(yn - 1, 1), SLOTS // yn, D), BF16), vm((SLOTS, D), BF16),
-        vm((NX, 288, W), F32), vm((NX, XN, PIECE, W), BF16), vm((NX, 3, 128, W), BF16), vm((NX, 3, 144, W), BF16),
-        vm((NX, 80, W), BF16), vm((NX, 64, W), BF16), vm((NX, 80, W), BF16), vm((NX, 64, W), BF16),
-        vm((NX, 4, 48, W), BF16), vm((NX, 4, 48, W), BF16),
-        vm((NZ, XN, 288, W), F32), vm((NZ, 4, XN, 48, W), BF16), vm((NZ, 4, XN, 48, W), BF16),
-        vm((NZ, 4, XN, 48, W), BF16), vm((NZ, 4, XN, 48, W), BF16), vm((NZ, XN, 48, W), BF16),
-        vm((NZ, 3, 32, W), BF16), vm((NZ, 3, 16, W), BF16),
+        [
+            [vm((XN, 288, w), F32)] + [vm((4, XN, 48, w), BF16)] * 4
+            + [vm((rows, w), BF16) for rows in (48, 48, 32, 16) * 2] for w in WIDTHS_Z
+        ],
+        [
+            [vm((288, w), F32)] + [vm((rows, w), BF16) for rows in (80, 64) * 2] + [vm((4, 48, w), BF16)] * 2
+            + [vm((rows, w), BF16) for rows in (PIECE, PIECE, 128, 144) * 2] for w in WIDTHS_X
+        ],
         pltpu.SemaphoreType.DMA((15,)), pltpu.SemaphoreType.DMA((3,)), pltpu.SemaphoreType.DMA((n_sem,)), pltpu.SemaphoreType.DMA((n_sem,)),
     ]
     encoded, mct, io, up_sum, down_sum = pl.pallas_call(
@@ -689,26 +699,26 @@
         decay_rate.reshape(1, HEADS), reset_depth.reshape(1, ROWS), out_proj, router.reshape(1, D),
         pad_vector.reshape(8, D // 8), up_weight, down_weight, cotangent,
     )
-    half = ROWS // 2
+    part = ROWS // 4
     return pl.pallas_call(
         finish,
-        grid=(2,),
+        grid=(4,),
         out_shape=(
             jax.ShapeDtypeStruct((ROWS, D), BF16),
             jax.ShapeDtypeStruct((ru, D), F32),
             jax.ShapeDtypeStruct((rd, D), F32),
         ),
         in_specs=[
-            pl.BlockSpec((half, D), lambda i: (i, 0)),
-            pl.BlockSpec((half, 2 * SLOTS), lambda i: (i, 0)),
+            pl.BlockSpec((part, D), lambda i: (i, 0)),
+            pl.BlockSpec((part, 2 * SLOTS), lambda i: (i, 0)),
             pl.BlockSpec((SLOTS, D), lambda i: (0, 0)),
-            pl.BlockSpec((ru // 2, D), lambda i: (i, 0)),
-            pl.BlockSpec((rd // 2, D), lambda i: (i, 0)),
+            pl.BlockSpec((ru // 4, D), lambda i: (i, 0)),
+            pl.BlockSpec((rd // 2, D), lambda i: (i // 2, 0)),
         ],
         out_specs=(
-            pl.BlockSpec((half, D), lambda i: (i, 0)),
-            pl.BlockSpec((ru // 2, D), lambda i: (i, 0)),
-            pl.BlockSpec((rd // 2, D), lambda i: (i, 0)),
+            pl.BlockSpec((part, D), lambda i: (i, 0)),
+            pl.BlockSpec((ru // 4, D), lambda i: (i, 0)),
+            pl.BlockSpec((rd // 2, D), lambda i: (i // 2, 0)),
         ),
         compiler_params=pltpu.CompilerParams(vmem_limit_bytes=60 * 2**20),
     )(encoded, mct, io, up_sum, down_sum)

time: 75.7 us -> 73.8 us (0.975)
  Pallas kernels: 74.4 us -> 72 us
    pallas_call x1, Pallas kernels: 71.5 us -> 67.9 us  [on_device(): pl.pallas_call(functools.partial(kernel, zn, yn), out_shape=(jax.ShapeDty...]
    pallas_call x1, Pallas kernels: 2.89 us -> 4.15 us  [on_device(): pl.pallas_call(finish, grid=(4,), out_shape=(jax.ShapeDtypeStruct((ROWS,...]
where the time goes in v4:
time: 73.8 us; the launch traced here: 72.7 us
  Pallas kernels  72 us (98%)
    pallas_call x1, Pallas kernels, on_device(): pl.pallas_call(functools.partial(kernel, zn, yn), out_shape=(jax.ShapeDty...  67.9 us
    pallas_call x1, Pallas kernels, on_device(): pl.pallas_call(finish, grid=(4,), out_shape=(jax.ShapeDtypeStruct((ROWS,...  4.15 us

profile of v4, /device:TPU:32, one launch (start us, length us, event | category | flops | bytes accessed | tf_op | source)
XLA Modules:
  0.0 72.7 jit_solution(3429683207961226915)
XLA Ops:
  0.6 67.9 %shard_map.166 = (bf16[512,1024]{1,0:T(8,128)(2,1)}, bf16[512,256]{1,0:T(8,128)(2,1)}, bf16[128,1024]{1,0:T(8,128)(2,1)}, f32[32,1024]{1,0:T(8,128)}, f32[16,1024]{1,0:T(8,128)}) custom-call(bf16[512,1024]{1,0:T(8,128)(2,1)} %tokens.1, s32[1,4096]{1,0:T(1,128)} %bitcast.8, bf16[1024,1024]{1,0:T(8,128)(2,1)} %value_proj.1, bf16[1024,128]{1,0:T(8,128)(2,1)} %write_proj.1, ...), custom_call_target="tpu_custom_call" | custom-call | tf_op jit(solution)/shard_map/pallas_call | solution.py:682
  68.5 4.2 %shard_map.167 = (bf16[512,1024]{1,0:T(8,128)(2,1)}, f32[32,1024]{1,0:T(8,128)}, f32[16,1024]{1,0:T(8,128)}) custom-call(bf16[512,1024]{1,0:T(8,128)(2,1)} %get-tuple-element.8.encoded, bf16[512,256]{1,0:T(8,128)(2,1)} %get-tuple-element.9.mct, bf16[128,1024]{1,0:T(8,128)(2,1)} %get-tuple-element.10.io, f32[32,1024]{1,0:T(8,128)} %get-tuple-element.11.up_sum, ...), custom_call_target="tpu_custom_call" | custom-call | tf_op jit(solution)/shard_map/pallas_call | solution.py:703

commit v5 on v4

--- a/solution.py
+++ b/solution.py
@@ -21,12 +21,12 @@
 SLOTS = 128
 XN, CN = 4, 2
 PLANE = XN * CN
-WIDTHS_Z, WIDTHS_X = (128, 128), (256, 256, 128, 128)
+WIDTHS_Z, WIDTHS_X = (256,), (256, 256, 128, 128)
 NZ, NQ = len(WIDTHS_Z), len(WIDTHS_Z + WIDTHS_X)
 ORDER = (
-    3, 0, 1, 2, 0, 1, 3, 0, 5, 1, 2, 3, 4, 1, 5, 0, 2, 3, 4, 1, 5, 0, 4, 2, 0, 3, 1, 5, 4, 1, 0, 2, 5, 4,
+    0, 3, 2, 0, 1, 3, 0, 2, 4, 1, 3, 0, 2, 3, 4, 1, 0, 4, 3, 2, 0, 1, 4, 0, 2, 1, 4,
 )
-SHARE_AT, STORE_AT = 3, 20
+SHARE_AT, STORE_AT = 7, 16
 PIECE = 272
 EPS = 1e-05
 G0, G1 = 0.7978845608028654, 0.044715
@@ -89,9 +89,10 @@
         copy.start()
 
     barrier = pltpu.get_barrier_semaphore()
-    partners = [(plane_at(lax.rem(me + o, PLANE)), y) for o in range(1, PLANE)]
+    partners = [
+        (plane_at(lax.rem(me + o, PLANE)), lax.rem(y + oy, yn)) for oy in range(yn) for o in range(PLANE) if o or oy
+    ]
     partners += [(lax.rem(z + o, zn) * PLANE + me, y) for o in range(1, zn)]
-    partners += [(seq, lax.rem(y + o, yn)) for o in range(1, yn)]
     for partner in partners:
         pl.semaphore_signal(barrier, inc=1, device_id=partner, device_id_type=MESH)
 
@@ -249,25 +250,17 @@
     def landing(j, at_y):
         return incoming.at[pl.ds(pl.multiple_of(j * 16, 16), 16), pl.ds(pl.multiple_of(at_y * qw, qw), qw)]
 
-    base = ids(PLANE + yn)
-    for o in range(1, PLANE):
-        j = lax.rem(me + o, PLANE)
-        step3.append(rdma(p3s.at[j], landing(me, y), base + o, plane_at(j), y))
-        step3[-1].start()
-        j = lax.rem(me - o + PLANE, PLANE)
-        from3.append(rdma(p3s.at[j], landing(j, y), base + o, plane_at(j), y))
+    base = ids(PLANE * yn)
+    for o in range(PLANE):
+        for oy in range(yn):
+            if o or oy:
+                i = base + o * yn + oy
+                j, at_y = lax.rem(me + o, PLANE), lax.rem(y + oy, yn)
+                step3.append(rdma(p3s.at[j], landing(me, y), i, plane_at(j), at_y))
+                step3[-1].start()
+                j, at_y = lax.rem(me - o + PLANE, PLANE), lax.rem(y - oy + yn, yn)
+                from3.append(rdma(p3s.at[j], landing(j, at_y), i, plane_at(j), at_y))
     incoming[pl.ds(pl.multiple_of(me * 16, 16), 16), mine] = p3s[me]
-
-    for copy in from3:
-        copy.wait_recv()
-    from3.clear()
-    for o in range(1, yn):
-        at_y = lax.rem(y + o, yn)
-        step3.append(rdma(incoming.at[:, mine], incoming.at[:, mine], base + PLANE + o, seq, at_y))
-        step3[-1].start()
-        at_y = lax.rem(y - o + yn, yn)
-        theirs = incoming.at[:, pl.ds(pl.multiple_of(at_y * qw, qw), qw)]
-        from3.append(rdma(theirs, theirs, base + PLANE + o, seq, at_y))
 
     for copy in loads[8:]:
         copy.wait()
@@ -422,21 +415,28 @@
             self.cut_r, self.cut_l = upper, lower
             self.up = {1: self.end_r, 2: self.near_r.at[0:upper, :], 3: self.near_l.at[lower:, :]}
             self.low = {1: self.near_r.at[upper:, :], 2: self.near_l.at[0:lower, :], 3: self.end_l}
-            self.base = ids(4)
+            self.base = ids(6)
 
         def ahead(self):
-            self.near = [
-                sent(self.near_r, self.near_r_in, self.base, right_x, y),
-                sent(self.near_l, self.near_l_in, self.base + 1, left_x, y),
+            i, far_r, far_l = self.base, slice(0, self.cut_r), slice(0, self.cut_l)
+            near_r, near_l = slice(self.cut_r, None), slice(self.cut_l, None)
+            self.far = [
+                sent(self.near_r.at[far_r, :], self.near_r_in.at[far_r, :], i, right_x, y),
+                sent(self.near_l.at[far_l, :], self.near_l_in.at[far_l, :], i + 1, left_x, y),
             ]
+            self.end = [
+                sent(self.near_r.at[near_r, :], self.near_r_in.at[near_r, :], i + 2, right_x, y),
+                sent(self.near_l.at[near_l, :], self.near_l_in.at[near_l, :], i + 3, left_x, y),
+            ]
 
         def later(self):
-            self.near[0].wait_recv()
+            i = self.base
+            self.far[0].wait_recv()
             self.end_r[...] = (f32(self.end_r[...]) + f32(self.near_r_in[0 : self.cut_r, :])).astype(BF16)
-            first = sent(self.end_r, self.end_r_in, self.base + 2, right_x, y)
-            self.near[1].wait_recv()
+            self.end.append(sent(self.end_r, self.end_r_in, i + 4, right_x, y))
+            self.far[1].wait_recv()
             self.end_l[...] = (f32(self.end_l[...]) + f32(self.near_l_in[0 : self.cut_l, :])).astype(BF16)
-            self.end = [first, sent(self.end_l, self.end_l_in, self.base + 3, left_x, y)]
+            self.end.append(sent(self.end_l, self.end_l_in, i + 5, left_x, y))
 
         def arrived(self):
             for copy in self.end:
@@ -652,7 +652,7 @@
     ru, rd, qw = 2 * D // sn, D // sn, D // yn
     n_pos = positions.shape[0]
     vm = pltpu.VMEM
-    n_sem = 2 * PLANE + zn + 4 + 3 * yn + NQ * 14
+    n_sem = PLANE + zn + PLANE * yn + 4 + 2 * yn + NQ * 14
     scratch = [
         vm((ROWS, D), BF16), vm((1, n_pos), jnp.int32), vm((D, D), BF16), vm((D, 2 * NS), BF16), vm((HEADS, D), BF16),
         vm((1, HEADS), F32), vm((1, HEADS), F32), vm((1, ROWS), F32), vm((D, D), BF16), vm((1, D), F32),
@@ -699,10 +699,10 @@
         decay_rate.reshape(1, HEADS), reset_depth.reshape(1, ROWS), out_proj, router.reshape(1, D),
         pad_vector.reshape(8, D // 8), up_weight, down_weight, cotangent,
     )
-    part = ROWS // 4
+    part = ROWS // 2
     return pl.pallas_call(
         finish,
-        grid=(4,),
+        grid=(2,),
         out_shape=(
             jax.ShapeDtypeStruct((ROWS, D), BF16),
             jax.ShapeDtypeStruct((ru, D), F32),
@@ -712,13 +712,13 @@
             pl.BlockSpec((part, D), lambda i: (i, 0)),
             pl.BlockSpec((part, 2 * SLOTS), lambda i: (i, 0)),
             pl.BlockSpec((SLOTS, D), lambda i: (0, 0)),
-            pl.BlockSpec((ru // 4, D), lambda i: (i, 0)),
-            pl.BlockSpec((rd // 2, D), lambda i: (i // 2, 0)),
+            pl.BlockSpec((ru // 2, D), lambda i: (i, 0)),
+            pl.BlockSpec((rd // 2, D), lambda i: (i, 0)),
         ],
         out_specs=(
             pl.BlockSpec((part, D), lambda i: (i, 0)),
-            pl.BlockSpec((ru // 4, D), lambda i: (i, 0)),
-            pl.BlockSpec((rd // 2, D), lambda i: (i // 2, 0)),
+            pl.BlockSpec((ru // 2, D), lambda i: (i, 0)),
+            pl.BlockSpec((rd // 2, D), lambda i: (i, 0)),
         ),
         compiler_params=pltpu.CompilerParams(vmem_limit_bytes=60 * 2**20),
     )(encoded, mct, io, up_sum, down_sum)

time: 73.8 us -> 68.5 us (0.928)
  Pallas kernels: 72 us -> 67.5 us
    pallas_call x1, Pallas kernels: 67.9 us -> 64.6 us  [on_device(): pl.pallas_call(functools.partial(kernel, zn, yn), out_shape=(jax.ShapeDty...]
    pallas_call x1, Pallas kernels: 4.15 us -> 2.89 us  [on_device(): pl.pallas_call(finish, grid=(2,), out_shape=(jax.ShapeDtypeStruct((ROWS,...]
where the time goes in v5:
time: 68.5 us; the launch traced here: 68.1 us
  Pallas kernels  67.5 us (99%)
    pallas_call x1, Pallas kernels, on_device(): pl.pallas_call(functools.partial(kernel, zn, yn), out_shape=(jax.ShapeDty...  64.6 us
    pallas_call x1, Pallas kernels, on_device(): pl.pallas_call(finish, grid=(2,), out_shape=(jax.ShapeDtypeStruct((ROWS,...  2.89 us

profile of v5, /device:TPU:32, one launch (start us, length us, event | category | flops | bytes accessed | tf_op | source)
XLA Modules:
  0.0 68.1 jit_solution(5455577849335693069)
XLA Ops:
  0.6 64.6 %shard_map.166 = (bf16[512,1024]{1,0:T(8,128)(2,1)}, bf16[512,256]{1,0:T(8,128)(2,1)}, bf16[128,1024]{1,0:T(8,128)(2,1)}, f32[32,1024]{1,0:T(8,128)}, f32[16,1024]{1,0:T(8,128)}) custom-call(bf16[512,1024]{1,0:T(8,128)(2,1)} %tokens.1, s32[1,4096]{1,0:T(1,128)} %bitcast.8, bf16[1024,1024]{1,0:T(8,128)(2,1)} %value_proj.1, bf16[1024,128]{1,0:T(8,128)(2,1)} %write_proj.1, ...), custom_call_target="tpu_custom_call" | custom-call | tf_op jit(solution)/shard_map/pallas_call | solution.py:682
  65.2 2.9 %shard_map.167 = (bf16[512,1024]{1,0:T(8,128)(2,1)}, f32[32,1024]{1,0:T(8,128)}, f32[16,1024]{1,0:T(8,128)}) custom-call(bf16[512,1024]{1,0:T(8,128)(2,1)} %get-tuple-element.8.encoded, bf16[512,256]{1,0:T(8,128)(2,1)} %get-tuple-element.9.mct, bf16[128,1024]{1,0:T(8,128)(2,1)} %get-tuple-element.10.io, f32[32,1024]{1,0:T(8,128)} %get-tuple-element.11.up_sum, ...), custom_call_target="tpu_custom_call" | custom-call | tf_op jit(solution)/shard_map/pallas_call | solution.py:703

commit v6 on v5

--- a/solution.py
+++ b/solution.py
@@ -26,7 +26,7 @@
 ORDER = (
     0, 3, 2, 0, 1, 3, 0, 2, 4, 1, 3, 0, 2, 3, 4, 1, 0, 4, 3, 2, 0, 1, 4, 0, 2, 1, 4,
 )
-SHARE_AT, STORE_AT = 7, 16
+SHARE_AT, STORE_AT = 12, 21
 PIECE = 272
 EPS = 1e-05
 G0, G1 = 0.7978845608028654, 0.044715

time: 68.5 us -> 68.5 us (level)
  no operation moved by 1% of the time
where the time goes in v6:
time: 68.5 us; the launch traced here: 68.1 us
  Pallas kernels  67.5 us (99%)
    pallas_call x1, Pallas kernels, on_device(): pl.pallas_call(functools.partial(kernel, zn, yn), out_shape=(jax.ShapeDty...  64.6 us
    pallas_call x1, Pallas kernels, on_device(): pl.pallas_call(finish, grid=(2,), out_shape=(jax.ShapeDtypeStruct((ROWS,...  2.89 us

profile of v6, /device:TPU:32, one launch (start us, length us, event | category | flops | bytes accessed | tf_op | source)
XLA Modules:
  0.0 68.1 jit_solution(9134124349234700195)
XLA Ops:
  0.6 64.6 %shard_map.166 = (bf16[512,1024]{1,0:T(8,128)(2,1)}, bf16[512,256]{1,0:T(8,128)(2,1)}, bf16[128,1024]{1,0:T(8,128)(2,1)}, f32[32,1024]{1,0:T(8,128)}, f32[16,1024]{1,0:T(8,128)}) custom-call(bf16[512,1024]{1,0:T(8,128)(2,1)} %tokens.1, s32[1,4096]{1,0:T(1,128)} %bitcast.8, bf16[1024,1024]{1,0:T(8,128)(2,1)} %value_proj.1, bf16[1024,128]{1,0:T(8,128)(2,1)} %write_proj.1, ...), custom_call_target="tpu_custom_call" | custom-call | tf_op jit(solution)/shard_map/pallas_call | solution.py:682
  65.2 2.9 %shard_map.167 = (bf16[512,1024]{1,0:T(8,128)(2,1)}, f32[32,1024]{1,0:T(8,128)}, f32[16,1024]{1,0:T(8,128)}) custom-call(bf16[512,1024]{1,0:T(8,128)(2,1)} %get-tuple-element.8.encoded, bf16[512,256]{1,0:T(8,128)(2,1)} %get-tuple-element.9.mct, bf16[128,1024]{1,0:T(8,128)(2,1)} %get-tuple-element.10.io, f32[32,1024]{1,0:T(8,128)} %get-tuple-element.11.up_sum, ...), custom_call_target="tpu_custom_call" | custom-call | tf_op jit(solution)/shard_map/pallas_call | solution.py:703
